TPU v7x, 32 devices: a whole 2x2x4 slice. The times are simulated.
32 devices in a mesh: expert: 8 (over y, x, core), tensor: 4 (over z).
Axes of the slice: x: 2, y: 2, z: 4, core: 2. Of those that a mesh axis runs over, the one named last changes fastest.
Arguments:
- patches: bfloat16 [3152, 768], P('expert'), may hold values from -6 to 6
- first_gain: float32 [768], replicated, may hold values from 0.5 to 1.5
- first_bias: float32 [768], replicated, may hold values from -1.5 to 1.5
- qkv_weight: bfloat16 [768, 3, 768], P(None, None, 'tensor'), may hold values from -0.3125 to 0.3125
- out_weight: bfloat16 [768, 768], P('tensor'), may hold values from -0.875 to 0.875
- second_gain: float32 [768], replicated, may hold values from 0.5 to 1.5
- second_bias: float32 [768], replicated, may hold values from -1.5 to 1.5
- router_weight: bfloat16 [768, 8], replicated, may hold values from -0.15625 to 0.15625
- up_weight: bfloat16 [8, 768, 3072], P('expert', None, 'tensor'), may hold values from -0.21875 to 0.21875
- down_weight: bfloat16 [8, 3072, 768], P('expert', 'tensor'), may hold values from -0.109375 to 0.109375
- expert_ids: int32 [3152, 2], P('expert'), may hold values from 0 to 7, all different within a row; in each aligned block of 394 rows (0 to 393, 394 to 787, ...) at most 148 rows name the same one
- router_noise: float32 [3152, 2], P('expert'), may hold values from -1.5 to 1.5
- images_live: int32 [8], P('expert'), may hold values from 1 to 2, as said below
- out_grad: bfloat16 [3152, 768], P('expert'), may hold values from -5 to 5
Outputs:
- block_out: bfloat16 [3152, 768], P('expert')
- patches_grad: float32 [3152, 768], P('expert')
- first_gain_grad: float32 [768], P('expert')
- first_bias_grad: float32 [768], P('expert')
- qkv_weight_grad: float32 [768, 3, 768], P('expert', None, 'tensor')
- out_weight_grad: float32 [768, 768], P('tensor', 'expert')
- second_gain_grad: float32 [768], P('expert')
- second_bias_grad: float32 [768], P('expert')
- router_weight_grad: float32 [768, 8], P('expert')
- up_weight_grad: float32 [8, 768, 3072], P('expert', None, 'tensor')
- down_weight_grad: float32 [8, 3072, 768], P('expert', 'tensor')
Inputs may be any that keep to these rules, and one draw needn't show every extreme that they name: `expert_ids`: the two experts of a row differ. Among the rows of one group no expert is named more than 148 times, and in every draw some expert is named exactly 148 times by the rows of some group. The first images_live[g] images of group g are in use, the rest are padding; every draw has a group with all 2 images in use and a group with the fewest.
All inputs are finite; a program needn't handle non-finite values.
Results may differ from a plain program's by a relative error of at most 0.015.
Values may be sent and summed in bfloat16 or wider, within the bound.
A program may use at most 128 MiB of HBM per device.

v0:
```python
import jax
import jax.numpy as jnp
from jax import lax
from jax.sharding import PartitionSpec as P

HEAD_DIM = 64
TOK_IMG = 197


epsilon = 1e-06


def layer_norm(values, norm_gain, norm_bias):
    center = values - jnp.mean(values, axis=-1, keepdims=True)
    variance = jnp.mean(center * center, axis=-1, keepdims=True)
    return center * lax.rsqrt(variance + epsilon) * norm_gain + norm_bias


def gelu_exact(values):
    return jax.nn.gelu(values, approximate=False)


def route_tables(expert_ids, images_live, row_count, expert_count, capacity):
    image_number = jnp.arange(row_count, dtype=jnp.int32) // TOK_IMG
    live_rows = (image_number < images_live[0]).astype(jnp.int32)
    ordered = jnp.concatenate([expert_ids[:, 0], expert_ids[:, 1]])
    live_pairs = jnp.concatenate([live_rows, live_rows])
    onehot = (ordered[:, None] == jnp.arange(expert_count, dtype=jnp.int32)[None, :]).astype(
        jnp.int32
    ) * live_pairs[:, None]
    earlier = jnp.cumsum(onehot, axis=0) - onehot
    slot_index = jnp.sum(earlier * onehot, axis=1)
    target = jnp.where(live_pairs > 0, ordered * capacity + slot_index, expert_count * capacity)
    return (target, live_rows.astype(jnp.float32))


def place_rows(first_rows, second_rows, target, expert_count, capacity):
    width_now = first_rows.shape[1]
    stacked = jnp.concatenate([first_rows, second_rows], axis=0)
    slotted = jnp.zeros((expert_count * capacity, width_now), first_rows.dtype)
    slotted = slotted.at[target].set(stacked, mode="drop")
    return slotted.reshape(expert_count, capacity, width_now)


def pick_rows(slotted, target, row_count):
    expert_count, capacity, width_now = slotted.shape
    padded = jnp.concatenate(
        [
            slotted.reshape(expert_count * capacity, width_now),
            jnp.zeros((1, width_now), slotted.dtype),
        ],
        axis=0,
    )
    picked = padded[target].astype(jnp.float32)
    return (picked[:row_count], picked[row_count:])


def send_out(slotted):
    return lax.all_to_all(slotted, "expert", split_axis=0, concat_axis=0, tiled=True)


def send_home(partial_sum):
    summed = lax.psum(partial_sum, "tensor").astype(jnp.bfloat16)
    return lax.all_to_all(summed, "expert", split_axis=0, concat_axis=0, tiled=True)


def on_device(
    patches,
    first_gain,
    first_bias,
    qkv_weight,
    out_weight,
    second_gain,
    second_bias,
    router_weight,
    up_weight,
    down_weight,
    expert_ids,
    router_noise,
    images_live,
    out_grad,
):
    row_count, model_width = patches.shape
    expert_count = router_weight.shape[1]
    capacity = (3 * row_count + expert_count - 1) // expert_count
    up_use, down_use = (up_weight[0], down_weight[0])

    def finish_rows(partial_sum):
        return send_home(partial_sum)

    local_width = out_weight.shape[0]
    local_heads = local_width // HEAD_DIM
    image_count = row_count // TOK_IMG
    scale_factor = HEAD_DIM ** (-0.5)
    target, live_rows = route_tables(expert_ids, images_live, row_count, expert_count, capacity)
    live_column = live_rows[:, None]
    inputs = patches.astype(jnp.float32)
    first_norm, first_back = jax.vjp(layer_norm, inputs, first_gain, first_bias)
    first_low = first_norm.astype(jnp.bfloat16)
    qkv_flat = qkv_weight.reshape(model_width, 3 * local_width)
    projected = jnp.dot(first_low, qkv_flat, preferred_element_type=jnp.float32).astype(
        jnp.bfloat16
    )
    projected = projected.reshape(image_count, TOK_IMG, 3, local_heads, HEAD_DIM)
    queries = projected[:, :, 0]
    key_rows = projected[:, :, 1]
    value_rows = projected[:, :, 2]
    scores = (
        jnp.einsum("ilhd,imhd->ihlm", queries, key_rows, preferred_element_type=jnp.float32)
        * scale_factor
    )
    highest_score = jnp.max(scores, axis=-1, keepdims=True)
    exponent = jnp.exp(scores - highest_score)
    totals = jnp.sum(exponent, axis=-1, keepdims=True)
    probs_low = (exponent / totals).astype(jnp.bfloat16)
    log_total = highest_score + jnp.log(totals)
    mixed = jnp.einsum("ihlm,imhd->ilhd", probs_low, value_rows, preferred_element_type=jnp.float32)
    mixed = mixed.astype(jnp.bfloat16).reshape(row_count, local_width)
    attended = lax.psum(jnp.dot(mixed, out_weight, preferred_element_type=jnp.float32), "tensor")
    resid = inputs + attended
    second_norm, second_back = jax.vjp(layer_norm, resid, second_gain, second_bias)
    second_low = second_norm.astype(jnp.bfloat16)
    logits = jnp.dot(second_low, router_weight, preferred_element_type=jnp.float32)
    selector = (
        expert_ids[:, :, None] == jnp.arange(expert_count, dtype=jnp.int32)[None, None, :]
    ).astype(jnp.float32)
    chosen = jnp.sum(selector * logits[:, None, :], axis=2) + router_noise
    gates = jax.nn.softmax(chosen, axis=-1)
    received = send_out(place_rows(second_low, second_low, target, expert_count, capacity))
    hidden_pre = jnp.einsum("scd,df->scf", received, up_use, preferred_element_type=jnp.float32)
    gelu_value, gelu_back = jax.vjp(gelu_exact, hidden_pre)
    activated = gelu_value.astype(jnp.bfloat16)
    expert_part = jnp.einsum("scf,fd->scd", activated, down_use, preferred_element_type=jnp.float32)
    first_out, second_out = pick_rows(finish_rows(expert_part), target, row_count)
    mixture = gates[:, 0:1] * first_out + gates[:, 1:2] * second_out
    block_out = (live_column * (resid + mixture)).astype(jnp.bfloat16)
    cotangent = out_grad.astype(jnp.float32) * live_column
    grad_first = (gates[:, 0:1] * cotangent).astype(jnp.bfloat16)
    grad_second = (gates[:, 1:2] * cotangent).astype(jnp.bfloat16)
    gate_grad = jnp.stack(
        [jnp.sum(cotangent * first_out, axis=1), jnp.sum(cotangent * second_out, axis=1)], axis=1
    )
    chosen_grad = gates * (gate_grad - jnp.sum(gates * gate_grad, axis=1, keepdims=True))
    logit_grad = jnp.sum(selector * chosen_grad[:, :, None], axis=1)
    router_grad = jnp.dot(
        second_low.astype(jnp.float32).T, logit_grad, precision=lax.Precision.HIGHEST
    )
    second_grad = jnp.dot(
        logit_grad, router_weight.astype(jnp.float32).T, precision=lax.Precision.HIGHEST
    )
    delta = send_out(place_rows(grad_first, grad_second, target, expert_count, capacity))
    down_grad = jnp.einsum("scf,scd->fd", activated, delta, preferred_element_type=jnp.float32)
    activated_grad = jnp.einsum("scd,fd->scf", delta, down_use, preferred_element_type=jnp.float32)
    hidden_grad = gelu_back(activated_grad)[0].astype(jnp.bfloat16)
    up_grad = jnp.einsum("scd,scf->df", received, hidden_grad, preferred_element_type=jnp.float32)
    input_part = jnp.einsum("scf,df->scd", hidden_grad, up_use, preferred_element_type=jnp.float32)
    first_back_rows, second_back_rows = pick_rows(finish_rows(input_part), target, row_count)
    second_grad = second_grad + first_back_rows + second_back_rows
    resid_grad, second_gain_grad, second_bias_grad = second_back(second_grad)
    resid_grad = resid_grad + cotangent
    attended_grad = resid_grad.astype(jnp.bfloat16)
    out_weight_grad = jnp.einsum(
        "rk,rd->kd", mixed, attended_grad, preferred_element_type=jnp.float32
    )
    mixed_grad = jnp.einsum(
        "rd,kd->rk", attended_grad, out_weight, preferred_element_type=jnp.float32
    ).astype(jnp.bfloat16)
    mixed_grad = mixed_grad.reshape(image_count, TOK_IMG, local_heads, HEAD_DIM)
    probs_again = jnp.exp(
        jnp.einsum("ilhd,imhd->ihlm", queries, key_rows, preferred_element_type=jnp.float32)
        * scale_factor
        - log_total
    )
    prob_grad = jnp.einsum(
        "ilhd,imhd->ihlm", mixed_grad, value_rows, preferred_element_type=jnp.float32
    )
    value_grad = jnp.einsum(
        "ihlm,ilhd->imhd",
        probs_again.astype(jnp.bfloat16),
        mixed_grad,
        preferred_element_type=jnp.float32,
    )
    score_grad = (
        probs_again * (prob_grad - jnp.sum(prob_grad * probs_again, axis=-1, keepdims=True))
    ).astype(jnp.bfloat16)
    query_grad = (
        jnp.einsum("ihlm,imhd->ilhd", score_grad, key_rows, preferred_element_type=jnp.float32)
        * scale_factor
    )
    key_grad = (
        jnp.einsum("ihlm,ilhd->imhd", score_grad, queries, preferred_element_type=jnp.float32)
        * scale_factor
    )
    projected_grad = (
        jnp.stack([query_grad, key_grad, value_grad], axis=2)
        .astype(jnp.bfloat16)
        .reshape(row_count, 3 * local_width)
    )
    qkv_grad = jnp.einsum(
        "rd,rk->dk", first_low, projected_grad, preferred_element_type=jnp.float32
    ).reshape(model_width, 3, local_width)
    first_part = jnp.einsum(
        "rk,dk->rd", projected_grad, qkv_flat, preferred_element_type=jnp.float32
    )
    first_grad = lax.psum(first_part.astype(jnp.bfloat16), "tensor").astype(jnp.float32)
    input_grad, first_gain_grad, first_bias_grad = first_back(first_grad)
    patches_grad = input_grad + resid_grad
    summed_grads = (
        lax.psum_scatter(first_gain_grad, "expert", scatter_dimension=0, tiled=True),
        lax.psum_scatter(first_bias_grad, "expert", scatter_dimension=0, tiled=True),
        lax.psum_scatter(qkv_grad, "expert", scatter_dimension=0, tiled=True),
        lax.psum_scatter(out_weight_grad.T, "expert", scatter_dimension=0, tiled=True),
        lax.psum_scatter(second_gain_grad, "expert", scatter_dimension=0, tiled=True),
        lax.psum_scatter(second_bias_grad, "expert", scatter_dimension=0, tiled=True),
        lax.psum_scatter(router_grad, "expert", scatter_dimension=0, tiled=True),
    )
    return (
        block_out,
        patches_grad,
        summed_grads[0],
        summed_grads[1],
        summed_grads[2],
        summed_grads[3].T,
        summed_grads[4],
        summed_grads[5],
        summed_grads[6],
        up_grad[None],
        down_grad[None],
    )


def solution(mesh):
    placed = (
        P("expert", None),
        P(),
        P(),
        P(None, None, "tensor"),
        P("tensor", None),
        P(),
        P(),
        P(),
        P("expert", None, "tensor"),
        P("expert", "tensor", None),
        P("expert", None),
        P("expert", None),
        P("expert"),
        P("expert", None),
    )
    return jax.shard_map(
        on_device,
        mesh=mesh,
        in_specs=placed,
        out_specs=(
            P("expert", None),
            P("expert", None),
            P("expert"),
            P("expert"),
            P("expert", None, "tensor"),
            P("tensor", "expert"),
            P("expert"),
            P("expert"),
            P("expert", None),
            P("expert", None, "tensor"),
            P("expert", "tensor", None),
        ),
        check_vma=False,
    )
```

profile of v0, /device:TPU:0, one launch (start us, length us, event | category | flops | bytes accessed | tf_op | source)
XLA Modules:
  0.0 667.5 jit_solution(6624331709048024399)
XLA Ops:
  8.6 1.4 fusion.15
  10.1 1.9 convolution_convert_fusion.1
  17.6 1.4 fusion.82
  19.8 2.0 reduce-window.6
  22.4 57.1 %all-reduce.13.cloned.1.call-done = f32[394,768]{1,0:T(8,128)} async-done(((f32[394,768]{1,0:T(8,128)}), f32[394,768]{1,0:T(8,128)}) %all-reduce.13.cloned.1.call-update) | async-done | bytes 1210384 | tf_op jit(solution)/shard_map/psum | solution.py:119
  79.6 1.5 fusion.77
  82.1 8.6 %scatter_custom_fusion = bf16[1184,768]{1,0:T(8,128)(2,1)} fusion(s32[788]{0:T(1024)S(1)} %get-tuple-element.67, bf16[394,768]{1,0:T(8,128)(2,1)S(1)} %add_convert_fusion.1, bf16[]{:T(256)} %constant.144, bf16[]{:T(256)} %constant.19.clone.1), kind=kCustom, calls=%fused_computation.68 | custom fusion | flops 2420736 | bytes 2433028 | tf_op jit(solution)/shard_map/scatter | solution.py:41
  90.8 2.6 reshape.270
  93.3 5.0 all-to-all-start
  100.1 12.7 %scatter_custom_fusion.1 = bf16[1184,768]{1,0:T(8,128)(2,1)S(1)} fusion(s32[788]{0:T(1024)S(1)} %get-tuple-element.67, bf16[394,768]{1,0:T(8,128)(2,1)} %get-tuple-element.87, bf16[]{:T(256)} %constant.144, bf16[394,768]{1,0:T(8,128)(2,1)} %get-tuple-element.86, bf16[]{:T(256)} %constant.19.clone.1), kind=kCustom, calls=%fused_computation.72 | custom fusion | flops 2420736 | bytes 3028996 | tf_op jit(solution)/shard_map/scatter | solution.py:41
  112.8 1.4 reshape.272
  114.2 8.3 %all-to-all-done = bf16[8,148,768]{2,1,0:T(8,128)(2,1)} async-done(((bf16[8,148,768]{2,1,0:T(8,128)(2,1)}), bf16[8,148,768]{2,1,0:T(8,128)(2,1)}, u32[]{:S(2)}, u32[]{:S(2)}) %all-to-all-start) | async-done | bytes 1818656 | tf_op jit(solution)/shard_map/all_to_all | solution.py:59
  122.5 3.8 all-to-all-start.2
  126.3 4.1 fusion.39
  130.4 1.8 copy-done.14
  132.2 9.3 %multiply_convert_fusion = (bf16[8,148,768]{2,1,0:T(8,128)(2,1)}, f32[8,148,768]{2,1,0:T(8,128)}) fusion(f32[8,148,768]{2,1,0:T(8,128)S(1)} %get-tuple-element.94, u8[148,768]{1,0:T(8,128)(4,1)S(1)} %get-tuple-element.56, u8[148,768]{1,0:T(8,128)(4,1)S(1)} %get-tuple-element.55), kind=kLoop, calls=%fused_computation.12 | loop fusion | flops 63651840 | bytes 9320448 | tf_op jit(solution)/shard_map/convert_element_type | solution.py:132
  141.6 8.9 %all-to-all-done.2 = bf16[8,148,768]{2,1,0:T(8,128)(2,1)S(1)} async-done(((bf16[8,148,768]{2,1,0:T(8,128)(2,1)}), bf16[8,148,768]{2,1,0:T(8,128)(2,1)S(1)}, u32[]{:S(2)}, u32[]{:S(2)}) %all-to-all-start.2) | async-done | bytes 1818656 | tf_op jit(solution)/shard_map/all_to_all | solution.py:59
  150.4 6.8 %add_convert_fusion = bf16[8,148,768]{2,1,0:T(8,128)(2,1)S(1)} fusion(f32[8,148,768]{2,1,0:T(8,128)} %get-tuple-element.79, f32[8,148,768]{2,1,0:T(8,128)} %copy-done.14, bf16[8,148,768]{2,1,0:T(8,128)(2,1)S(1)} %all-to-all-done.2, bf16[1,768,768]{2,1,0:T(8,128)(2,1)} %param.23), kind=kOutput, calls=%fused_computation.11 | convolution fusion | flops 1409433600 | bytes 12091392 | tf_op jit(solution)/shard_map/scd,fd->scf/dot_general | solution.py:153
  157.3 3.5 fusion.31
  160.8 3.5 fusion.29
  164.3 250.0 %all-reduce.16 = (bf16[8,148,768]{2,1,0:T(8,128)(2,1)}, bf16[8,148,768]{2,1,0:T(8,128)(2,1)}) all-reduce(f32[8,148,768]{2,1,0:T(8,128)} %fusion.29, f32[8,148,768]{2,1,0:T(8,128)} %fusion.31), channel_id=1, replica_groups=mesh['expert'=8,'tensor'=4] {'tensor'}, use_global_device_ids=true, to_apply=%region_14.15 | all-reduce | flops 1818624 | bytes 10911744 | tf_op jit(solution)/shard_map/psum | solution.py:63
  414.3 31.3 %all_to_all.20 = bf16[8,148,768]{2,1,0:T(8,128)(2,1)S(1)} all-to-all(bf16[8,148,768]{2,1,0:T(8,128)(2,1)} %get-tuple-element.73), channel_id=1, replica_groups=mesh['expert'=8,'tensor'=4] {'expert'}, dimensions={0} | all-to-all | bytes 3637248 | tf_op jit(solution)/shard_map/all_to_all | solution.py:64
  445.6 4.3 all-to-all-start.1
  450.2 1.4 reshape.273
  451.6 1.6 concatenate.54
  453.2 20.9 %all-to-all-done.1 = bf16[8,148,768]{2,1,0:T(8,128)(2,1)} async-done(((bf16[8,148,768]{2,1,0:T(8,128)(2,1)}), bf16[8,148,768]{2,1,0:T(8,128)(2,1)}, u32[]{:S(2)}, u32[]{:S(2)}) %all-to-all-start.1) | async-done | bytes 1818656 | tf_op jit(solution)/shard_map/all_to_all | solution.py:64
  474.1 2.6 reshape.271
  476.7 2.8 concatenate.52
  479.5 4.1 gather_fusion.1
  483.6 6.5 gather_fusion
  490.1 1.6 convert_element_type.121
  491.9 1.6 multiply_reduce_fusion.4
  493.5 1.7 fusion.85
  495.2 1.5 convert_element_type.128
  504.3 1.5 convolution_convert_fusion
  507.6 2.4 fusion.45
  511.9 5.4 convolution_bitcast_fusion
  517.3 4.7 convolution_bitcast_fusion.1
  522.0 11.8 %reduce-scatter.10.cloned.1.call-done = f32[96,8]{1,0:T(8,128)} async-done(((f32[768,8]{1,0:T(8,128)}), f32[96,8]{1,0:T(8,128)}) %reduce-scatter.10.cloned.1.call-update) | async-done | bytes 3088
  533.8 1.5 copy.96
  535.2 40.7 %all-reduce.15.cloned.1.call-done = bf16[394,768]{1,0:T(8,128)(2,1)} async-done(((bf16[394,768]{1,0:T(8,128)(2,1)}), bf16[394,768]{1,0:T(8,128)(2,1)}) %all-reduce.15.cloned.1.call-update) | async-done | bytes 605200 | tf_op jit(solution)/shard_map/psum | solution.py:205
  575.9 1.5 convert_reduce_fusion
  577.4 1.9 fusion.17
  579.3 23.9 %all-reduce.7 = (f32[768]{0:T(1024)S(1)}, f32[768]{0:T(1024)S(1)}, f32[768]{0:T(1024)S(1)}, f32[768]{0:T(1024)S(1)}) all-reduce(f32[768]{0:T(1024)S(1)} %get-tuple-element.61, f32[768]{0:T(1024)S(1)} %get-tuple-element.64, f32[768]{0:T(1024)S(1)} %get-tuple-element.59, ...), channel_id=2, replica_groups=mesh['expert'=8,'tensor'=4] {'expert'}, use_global_device_ids=true, to_apply=%region_28.29.clone | all-reduce | flops 3072 | bytes 24576
  605.5 3.0 add_add_fusion.2
  608.5 5.4 reduce-scatter.8.cloned.1.call-done
  613.9 1.6 copy.90
  615.6 45.0 %reduce-scatter.6.cloned.1.call-done = f32[96,3,192]{2,0,1:T(8,128)} async-done(((f32[768,3,192]{2,0,1:T(8,128)}), f32[96,3,192]{2,0,1:T(8,128)}) %reduce-scatter.6.cloned.1.call-update) | async-done | bytes 221200 | tf_op jit(solution)/shard_map/reduce_scatter | solution.py:211
  (146 shorter events, 23.8 us)
Async XLA Ops:
  7.2 119.1 %copy-start = (bf16[1,768,768]{2,1,0:T(8,128)(2,1)S(1)}, bf16[1,768,768]{2,1,0:T(8,128)(2,1)}, u32[]{:S(2)}) copy-start(bf16[1,768,768]{2,1,0:T(8,128)(2,1)} %param.22) | copy-start | bytes 3538948
  7.2 2.8 copy-start.6
  7.2 2.8 copy-start.25
  7.2 2.8 copy-start.32
  7.2 72.4 %all-reduce.13.cloned.1.call-start = ((), (), s32[]{:S(2)}) async-start(), calls=%async_computation.7 | async-start | bytes 2457600 | tf_op jit(solution)/shard_map/psum | solution.py:119
  14.0 1.5 copy-start.19
  14.2 2.1 copy-start.22
  15.7 0.7 copy-start.17
  16.1 1.1 copy-start.2
  16.4 1.2 copy-start.20
  17.6 2.1 copy-start.24
  81.1 1.0 copy-start.4
  81.1 0.7 copy-start.26
  81.1 0.7 copy-start.28
  82.1 16.3 %copy-start.10 = (bf16[394,768]{1,0:T(8,128)(2,1)}, bf16[394,768]{1,0:T(8,128)(2,1)S(1)}, u32[]{:S(2)}) copy-start(bf16[394,768]{1,0:T(8,128)(2,1)S(1)} %add_convert_fusion.1) | copy-start | bytes 1815556
  93.3 5.0 copy-start.27
  93.3 5.4 copy-start.29
  93.3 5.4 copy-start.12
  93.3 29.2 %all-to-all-start = ((bf16[8,148,768]{2,1,0:T(8,128)(2,1)}), bf16[8,148,768]{2,1,0:T(8,128)(2,1)}, u32[]{:S(2)}, u32[]{:S(2)}) async-start(bf16[8,148,768]{2,1,0:T(8,128)(2,1)} %reshape.270), calls=%async_computation | async-start | bytes 3735552 | tf_op jit(solution)/shard_map/all_to_all | solution.py:59
  122.5 27.9 %all-to-all-start.2 = ((bf16[8,148,768]{2,1,0:T(8,128)(2,1)}), bf16[8,148,768]{2,1,0:T(8,128)(2,1)S(1)}, u32[]{:S(2)}, u32[]{:S(2)}) async-start(bf16[8,148,768]{2,1,0:T(8,128)(2,1)} %reshape.272), calls=%async_computation.2 | async-start | bytes 3735552 | tf_op jit(solution)/shard_map/all_to_all | solution.py:59
  130.4 1.9 copy-start.14
  150.4 6.8 %copy-start.15 = (bf16[8,148,768]{2,1,0:T(8,128)(2,1)}, bf16[8,148,768]{2,1,0:T(8,128)(2,1)S(1)}, u32[]{:S(2)}) copy-start(bf16[8,148,768]{2,1,0:T(8,128)(2,1)S(1)} %all-to-all-done.2) | copy-start | bytes 5455876
  157.3 3.6 copy-start.34
  157.3 3.5 copy-start.16
  157.3 3.5 copy-start.30
  445.6 28.5 %all-to-all-start.1 = ((bf16[8,148,768]{2,1,0:T(8,128)(2,1)}), bf16[8,148,768]{2,1,0:T(8,128)(2,1)}, u32[]{:S(2)}, u32[]{:S(2)}) async-start(bf16[8,148,768]{2,1,0:T(8,128)(2,1)} %get-tuple-element.72), calls=%async_computation.1 | async-start | bytes 3735552 | tf_op jit(solution)/shard_map/all_to_all | solution.py:64
  449.9 83.9 %reduce-scatter.10.cloned.1.call-start = ((), (), s32[]{:S(2)}) async-start(), calls=%async_computation.11 | async-start | bytes 442368
  490.0 1.7 copy-start.5
  490.1 1.8 copy-start.13
  491.9 1.6 copy-start.11
  498.6 1.0 copy-start.8
  498.6 1.2 copy-start.21
  499.7 1.3 copy-start.3
  500.1 1.2 copy-start.23
  501.8 0.9 copy-start.18
  503.0 72.9 %all-reduce.15.cloned.1.call-start = ((), (), s32[]{:S(2)}) async-start(), calls=%async_computation.8 | async-start | bytes 1228800 | tf_op jit(solution)/shard_map/psum | solution.py:205
  503.2 1.2 copy-start.31
  505.9 1.7 copy-start.7
  505.9 108.0 %reduce-scatter.8.cloned.1.call-start = ((), (), s32[]{:S(2)}) async-start(), calls=%async_computation.10 | async-start | bytes 884736 | tf_op jit(solution)/shard_map/reduce_scatter | solution.py:212
  507.3 153.3 %reduce-scatter.6.cloned.1.call-start = ((), (), s32[]{:S(2)}) async-start(), calls=%async_computation.9 | async-start | bytes 2654208 | tf_op jit(solution)/shard_map/reduce_scatter | solution.py:211
  510.0 0.7 copy-start.33
  511.9 5.4 copy-start.35
  535.2 70.3 %copy-start.9 = (f32[394,768]{1,0:T(8,128)S(1)}, f32[394,768]{1,0:T(8,128)}, u32[]{:S(2)}) copy-start(f32[394,768]{1,0:T(8,128)} %copy-done.8) | copy-start | bytes 3631108
  605.5 55.0 %copy-start.1 = (bf16[1,768,768]{2,1,0:T(8,128)(2,1)S(1)}, bf16[1,768,768]{2,1,0:T(8,128)(2,1)}, u32[]{:S(2)}) copy-start(bf16[1,768,768]{2,1,0:T(8,128)(2,1)} %param.22) | copy-start | bytes 3538948
Sparse Core Ops, SparseCore 0:
  19.1 60.4 all-reduce.12
  503.1 30.6 reduce-scatter.9
  536.2 39.5 all-reduce.14
  579.2 34.6 reduce-scatter.7
  618.1 42.4 reduce-scatter.5
where the time goes:
time: 676 us; the launch traced here: 668 us
  blocking collectives  305 us (45%)
  waiting for transfers between devices  198 us (29%)
  other arithmetic  51.8 us (8%)
  matrix products  42.2 us (6%)
  local copies, waits for them, and re-layouts  40.3 us (6%)
  between operations  16.2 us (2%)
  starting transfers between devices  13.7 us (2%)
    psum x1, blocking collectives, send_home(): summed = lax.psum(partial_sum, 'tensor').astype(jnp.bfloat16)  250 us
    psum x1, waiting for transfers between devices, on_device(): lax.psum(jnp.dot(mixed, out_weight, preferred_element_type=jnp.float32),...  57.1 us
    reduce_scatter x1, waiting for transfers between devices, on_device(): lax.psum_scatter(qkv_grad, 'expert', scatter_dimension=0, tiled=True)  45 us
    psum x1, waiting for transfers between devices, on_device(): lax.psum(first_part.astype(jnp.bfloat16), 'tensor').astype(jnp.float32)  40.7 us
    all_to_all x1, blocking collectives, send_home(): lax.all_to_all(summed, 'expert', split_axis=0, concat_axis=0, tiled=True)  31.3 us
    unnamed x1, blocking collectives  23.9 us
    scatter x2, other arithmetic, place_rows(): slotted = slotted.at[target].set(stacked, mode='drop')  21.3 us
    all_to_all x1, waiting for transfers between devices, send_home(): lax.all_to_all(summed, 'expert', split_axis=0, concat_axis=0, tiled=True)  20.9 us
  transfers between devices with their start and end apart: 8, of which 8 were waited for; matrix products, arithmetic and copies ran while one was open for 10% of the time, Pallas kernels for 0%

commit v1 on v0

v1 whole, which is shorter than its diff:
```python
import functools

import jax
import jax.numpy as jnp
from jax import lax
from jax.experimental import pallas as pl
from jax.experimental.pallas import tpu as pltpu
from jax.sharding import PartitionSpec as P

HEAD_DIM = 64
TOK_IMG = 197
TILE = 16
EPSILON = 1e-06
MESH = pl.DeviceIdType.MESH
F32 = jnp.float32
BF16 = jnp.bfloat16


def round_up(value, unit):
    return (value + unit - 1) // unit * unit


def nn(a, b):
    return lax.dot_general(a, b, (((1,), (0,)), ((), ())), preferred_element_type=F32)


def nt(a, b):
    return lax.dot_general(a, b, (((1,), (1,)), ((), ())), preferred_element_type=F32)


def tn(a, b):
    return lax.dot_general(a, b, (((0,), (0,)), ((), ())), preferred_element_type=F32)


def in_three(values):
    high = values.astype(BF16)
    rest = values - high.astype(F32)
    middle = rest.astype(BF16)
    return high, middle, (rest - middle.astype(F32)).astype(BF16)


def normalize(values):
    center = values - jnp.mean(values, axis=-1, keepdims=True)
    scale = lax.rsqrt(jnp.mean(center * center, axis=-1, keepdims=True) + EPSILON)
    return center * scale, scale


def norm_back(normal, scale, grad_normal):
    return scale * (
        grad_normal
        - jnp.mean(grad_normal, axis=-1, keepdims=True)
        - normal * jnp.mean(grad_normal * normal, axis=-1, keepdims=True)
    )


class Shapes:
    def __init__(self, mesh, row_count, model_width, local_width):
        self.experts = mesh.shape["expert"]
        self.depth = mesh.shape["tensor"]
        self.rows = row_count
        self.width = model_width
        self.local = local_width
        self.heads = local_width // HEAD_DIM
        self.padded = round_up(row_count, TILE)
        self.capacity = (3 * row_count + self.experts - 1) // self.experts
        self.slots = round_up(self.capacity, TILE)
        self.slot_lanes = round_up(self.slots, 128)
        self.step = (self.padded - TILE) // self.depth
        self.window = self.step + TILE
        self.share = model_width // self.experts
        self.share_rows = round_up(self.share, TILE)
        self.small = round_up(self.experts + 4, 8)


def whole_kernel(
    sh,
    patches,
    gain1,
    bias1,
    wqkv,
    wout,
    gain2,
    bias2,
    router_t,
    ids_row,
    noise_row,
    images_live,
    out_grad,
    up_hbm,
    down_hbm,
    block_out,
    patches_grad,
    qkv_out,
    wout_out,
    small_out,
    up_out,
    down_out,
    up,
    down,
    wfull,
    pt,
    og,
    first_low,
    q_s,
    k_s,
    v_s,
    probs_s,
    mixed_all,
    resid,
    second_low,
    place,
    x_send,
    x_recv,
    c_send,
    c_recv,
    g_send,
    g_recv,
    act,
    slope,
    delta,
    hid,
    eo_send,
    eo_home,
    ei_home,
    gg_send,
    gg_home,
    acc,
    mix_part,
    mix_recv,
    in_part,
    in_recv,
    first_recv,
    rterm,
    resid_win,
    bo_all,
    ag_all,
    pg_all,
    at_grad,
    gz_send,
    gz_recv,
    qg_send,
    qg_recv,
    og_wsend,
    og_wrecv,
    sz_send,
    sz_recv,
    sp_send,
    sp_recv,
    fz_send,
    fz_recv,
    fp_send,
    fp_recv,
    local_sem,
    e_sem,
    z_sem,
    z_extra,
    w_sem,
):
    E, Z = sh.experts, sh.depth
    R, RP, D = sh.rows, sh.padded, sh.width
    CP, CL = sh.slots, sh.slot_lanes
    me = lax.axis_index("expert")
    mz = lax.axis_index("tensor")

    def plane(step):
        return lax.rem(me + step, E)

    def before(step):
        return lax.rem(me - step + E, E)

    def above(step):
        return lax.rem(mz + step, Z)

    def below(step):
        return lax.rem(mz - step + Z, Z)

    def to_plane(src, dst, kind, step):
        return pltpu.make_async_remote_copy(
            src_ref=src,
            dst_ref=dst,
            send_sem=e_sem.at[kind, 0, step],
            recv_sem=e_sem.at[kind, 1, step],
            device_id=(plane(step), mz),
            device_id_type=MESH,
        )

    def to_depth(src, dst, kind, step, sems=None):
        sems = z_sem if sems is None else sems
        return pltpu.make_async_remote_copy(
            src_ref=src,
            dst_ref=dst,
            send_sem=sems.at[kind, 0, step],
            recv_sem=sems.at[kind, 1, step],
            device_id=(me, above(step)),
            device_id_type=MESH,
        )

    barrier = pltpu.get_barrier_semaphore()
    for step in range(1, E):
        pl.semaphore_signal(barrier, inc=1, device_id=(plane(step), mz), device_id_type=MESH)
    for step in range(1, Z):
        pl.semaphore_signal(barrier, inc=1, device_id=(me, above(step)), device_id_type=MESH)

    load_up = pltpu.make_async_copy(up_hbm, up, local_sem.at[0])
    load_down = pltpu.make_async_copy(down_hbm, down, local_sem.at[1])
    load_up.start()
    load_down.start()

    live_rows = images_live[0] * TOK_IMG
    lane = lax.broadcasted_iota(jnp.int32, (1, RP), 1)
    live = (lane < live_rows).astype(F32)
    expert_of = lax.broadcasted_iota(jnp.int32, (E, RP), 0)
    ids = ids_row[...]
    hot = [(expert_of == ids[k : k + 1]).astype(F32) * live for k in range(2)]
    earlier = (
        lax.broadcasted_iota(jnp.int32, (RP, RP), 0) < lax.broadcasted_iota(jnp.int32, (RP, RP), 1)
    ).astype(BF16)
    counts = [nn(h.astype(BF16), earlier) for h in hot]
    counts[1] = counts[1] + jnp.sum(hot[0], axis=1, keepdims=True)
    start = expert_of.astype(F32) * CP
    spot_row = [
        jnp.where(live > 0, jnp.sum(hot[k] * (counts[k] + start), axis=0, keepdims=True), -1.0)
        for k in range(2)
    ]
    spot_row = [s.astype(jnp.int32) for s in spot_row]
    eye_rows = lax.broadcasted_iota(jnp.int32, (RP, RP), 0) == lax.broadcasted_iota(
        jnp.int32, (RP, RP), 1
    )
    spot_col = [
        jnp.sum(jnp.where(eye_rows, s.astype(F32), 0.0), axis=1, keepdims=True).astype(jnp.int32)
        for s in spot_row
    ]
    slot_lane = lax.broadcasted_iota(jnp.int32, (RP, E * CP), 1)
    place[...] = ((slot_lane == spot_col[0]) | (slot_lane == spot_col[1])).astype(BF16)

    def spread(e):
        slot = lax.broadcasted_iota(jnp.int32, (CP, RP), 0) + e * CP
        return slot == spot_row[0], slot == spot_row[1]

    eye_slots = lax.broadcasted_iota(jnp.int32, (CP, CL), 0) == lax.broadcasted_iota(
        jnp.int32, (CP, CL), 1
    )

    def as_row(column):
        return jnp.sum(jnp.where(eye_slots, column, 0.0), axis=0, keepdims=True)

    def as_column(row):
        return jnp.sum(jnp.where(eye_slots, row, 0.0), axis=1, keepdims=True)

    row_of = lax.broadcasted_iota(jnp.int32, (R, 1), 0)
    og[pl.ds(RP - TILE, TILE)] = jnp.zeros((TILE, D), BF16)
    og[0:R] = jnp.where(row_of < live_rows, out_grad[...], jnp.zeros((), BF16))
    pt[pl.ds(RP - TILE, TILE)] = jnp.zeros((TILE, D), BF16)
    pt[0:R] = patches[...]

    def pack_cotangent(e, carry):
        s0, s1 = spread(e)
        c_send[e] = nn((s0 | s1).astype(BF16), og[...]).astype(BF16)
        return carry

    lax.fori_loop(0, E, pack_cotangent, 0)

    pl.semaphore_wait(barrier, E - 1 + Z - 1)

    half = D // 2
    core = lax.rem(me, 2)
    sibling = me + 1 - 2 * core
    columns = pl.ds(pl.multiple_of(core * half, 128), half)
    wfull[mz] = wout[...]
    w_out_copies = []
    for step in range(1, Z):
        copy = to_depth(wout.at[:, columns], wfull.at[mz, :, columns], 0, step)
        copy.start()
        w_out_copies.append(copy)
    c_copies = []
    for step in range(1, E):
        copy = to_plane(c_send.at[plane(step)], c_recv.at[me], 0, step)
        copy.start()
        c_copies.append(copy)
    c_recv[me] = c_send[me]

    normal, _ = normalize(pt[...].astype(F32))
    first_low[...] = (normal * gain1[...].reshape(1, D) + bias1[...].reshape(1, D)).astype(BF16)
    projected = nn(first_low[...], wqkv[...]).astype(BF16)
    for h in range(sh.heads):
        for part, dest in enumerate((q_s, k_s, v_s)):
            begin = part * sh.local + h * HEAD_DIM
            dest[h] = projected[:, begin : begin + HEAD_DIM]
    row2 = lax.broadcasted_iota(jnp.int32, (RP, RP), 0)
    col2 = lax.broadcasted_iota(jnp.int32, (RP, RP), 1)
    same = ((row2 >= TOK_IMG) == (col2 >= TOK_IMG)) & (col2 < R)
    scale = HEAD_DIM ** (-0.5)
    heads = []
    for h in range(sh.heads):
        scores = jnp.where(same, nt(q_s[h], k_s[h]) * scale, -1e30)
        exponent = jnp.exp(scores - jnp.max(scores, axis=1, keepdims=True))
        probs = exponent / jnp.sum(exponent, axis=1, keepdims=True)
        probs_s[h] = probs
        heads.append(nn(probs.astype(BF16), v_s[h]).astype(BF16))
    mixed_all[mz] = jnp.concatenate(heads, axis=1)
    m_copies = []
    for step in range(1, Z):
        copy = to_depth(mixed_all.at[mz], mixed_all.at[mz], 1, step)
        copy.start()
        m_copies.append(copy)

    w_passed = []
    for step in range(1, Z):
        origin = below(step)
        w_out_copies[step - 1].wait_recv()
        copy = pltpu.make_async_remote_copy(
            src_ref=wfull.at[origin, :, columns],
            dst_ref=wfull.at[origin, :, columns],
            send_sem=w_sem.at[0, step],
            recv_sem=w_sem.at[1, step],
            device_id=(sibling, mz),
            device_id_type=MESH,
        )
        copy.start()
        w_passed.append(copy)
    for copy in w_passed:
        copy.wait_recv()

    resid[...] = pt[...].astype(F32) + nn(mixed_all[mz], wfull[mz])
    for step in range(1, Z):
        m_copies[step - 1].wait_recv()
        resid[...] += nn(mixed_all[below(step)], wfull[below(step)])

    normal, _ = normalize(resid[...])
    second_low[...] = (normal * gain2[...].reshape(1, D) + bias2[...].reshape(1, D)).astype(BF16)
    logits = nt(router_t[...], second_low[...])
    chosen = [
        jnp.sum(hot[k] * logits, axis=0, keepdims=True) + noise_row[k : k + 1, :] for k in range(2)
    ]
    top = jnp.maximum(chosen[0], chosen[1])
    powers = [jnp.exp(c - top) for c in chosen]
    gates = [p / (powers[0] + powers[1]) for p in powers]

    def pack_rows(e, carry):
        s0, s1 = spread(e)
        x_send[e] = nn((s0 | s1).astype(BF16), second_low[...]).astype(BF16)
        gate = jnp.sum(
            jnp.where(s0, gates[0], 0.0) + jnp.where(s1, gates[1], 0.0), axis=1, keepdims=True
        )
        g_send[e] = jnp.broadcast_to(as_row(gate), (8, CL))
        return carry

    lax.fori_loop(0, E, pack_rows, 0)
    for step in range(1, E):
        to_plane(g_send.at[plane(step)], g_recv.at[me], 1, step).start()
        to_plane(x_send.at[plane(step)], x_recv.at[me], 2, step).start()
    g_recv[me] = g_send[me]
    x_recv[me] = x_send[me]

    load_up.wait()
    load_down.wait()

    def forward(step, carry):
        group = before(step)

        @pl.when(step > 0)
        def _():
            to_plane(g_send.at[0], g_recv.at[group], 1, step).wait_recv()
            to_plane(x_send.at[0], x_recv.at[group], 2, step).wait_recv()
            to_plane(c_send.at[0], c_recv.at[group], 0, step).wait_recv()

        hidden = nn(x_recv[group], up[...])
        below_it = 0.5 * (1.0 + lax.erf(hidden * (0.5**0.5)))
        bell = jnp.exp(-0.5 * hidden * hidden) * 0.3989422804014327
        act[group] = (hidden * below_it).astype(BF16)
        slope[group] = (below_it + hidden * bell).astype(BF16)
        result = nn(act[group], down[...])
        gate = as_column(g_recv[group][0:1])
        given = c_recv[group].astype(F32)
        dots = jnp.sum(given * result, axis=1, keepdims=True)
        gg_send[group] = jnp.broadcast_to(as_row(dots), (8, CL))
        eo_send[group] = (gate * result).astype(BF16)
        delta[group] = (gate * given).astype(BF16)

        @pl.when(step > 0)
        def _():
            back_to(gg_send.at[group], gg_home.at[me], 3, step).start()
            back_to(eo_send.at[group], eo_home.at[me], 4, step).start()

        return carry

    def back_to(src, dst, kind, step):
        return pltpu.make_async_remote_copy(
            src_ref=src,
            dst_ref=dst,
            send_sem=e_sem.at[kind, 0, step],
            recv_sem=e_sem.at[kind, 1, step],
            device_id=(before(step), mz),
            device_id_type=MESH,
        )

    lax.fori_loop(0, E, forward, 0)
    gg_home[me] = gg_send[me]
    eo_home[me] = eo_send[me]

    for copy in c_copies:
        copy.wait_send()
    ei_send = c_send

    def backward(step, carry):
        group = before(step)
        hid[group] = (nt(delta[group], down[...]) * slope[group]).astype(BF16)
        ei_send[group] = nt(hid[group], up[...]).astype(BF16)

        @pl.when(step > 0)
        def _():
            back_to(ei_send.at[group], ei_home.at[me], 5, step).start()

        return carry

    lax.fori_loop(0, E, backward, 0)
    ei_home[me] = ei_send[me]

    strip = 128
    F = up.shape[1]

    def flat(ref, first, size):
        return ref[:, :, pl.ds(pl.multiple_of(first, 128), size)].reshape(E * CP, size)

    def strip_copy(i, out, slot):
        return pltpu.make_async_copy(
            acc.at[slot], out.at[pl.ds(pl.multiple_of(i * strip, strip), strip)], local_sem.at[slot]
        )

    def strips(out, lhs, rhs, count, slot):
        def one(i, carry):
            at = slot + lax.rem(i, 2)

            @pl.when(i >= 2)
            def _():
                strip_copy(i - 2, out, at).wait()

            acc[at] = tn(flat(lhs, i * strip, strip), flat(rhs, 0, rhs.shape[2]))
            strip_copy(i, out, at).start()
            return carry

        lax.fori_loop(0, count, one, 0)

    strips(up_out, x_recv, hid, D // strip, 0)
    strips(down_out, act, delta, F // strip, 2)

    S, W = sh.step, sh.window

    def tail_of(position):
        return pl.ds(pl.multiple_of(position * S + TILE, TILE), S)

    def window_of(position):
        return pl.ds(pl.multiple_of(position * S, TILE), W)

    def scatter_windows(part, recv, kind):
        for step in range(1, Z):
            target = above(step)
            to_depth(
                part.at[tail_of(target)], recv.at[mz, pl.ds(TILE, S)], kind, step
            ).start()

            @pl.when(target == 0)
            def _():
                to_depth(
                    part.at[pl.ds(0, TILE)], recv.at[mz, pl.ds(0, TILE)], kind, step, z_extra
                ).start()

    def wait_scatter(part, recv, kind, total):
        for step in range(1, Z):
            source = below(step)
            to_depth(
                part.at[tail_of(0)], recv.at[source, pl.ds(TILE, S)], kind, step
            ).wait_recv()

            @pl.when(mz == 0)
            def _():
                to_depth(
                    part.at[pl.ds(0, TILE)], recv.at[source, pl.ds(0, TILE)], kind, step, z_extra
                ).wait_recv()

            total = total + recv[source].astype(F32)
        return total

    def finish_scatter(part, recv, kind):
        for step in range(1, Z):
            to_depth(
                part.at[tail_of(0)], recv.at[mz, pl.ds(TILE, S)], kind, step
            ).wait_send()

            @pl.when(above(step) == 0)
            def _():
                to_depth(
                    part.at[pl.ds(0, TILE)], recv.at[mz, pl.ds(0, TILE)], kind, step, z_extra
                ).wait_send()

    def gather_windows(every, kind):
        for step in range(1, Z):
            tail = every.at[mz, pl.ds(TILE, S)]
            to_depth(tail, tail, kind, step).start()

            @pl.when(mz == 0)
            def _():
                head = every.at[mz, pl.ds(0, TILE)]
                to_depth(head, head, kind, step, z_extra).start()

    def wait_gather(every, kind):
        for step in range(1, Z):
            source = below(step)
            tail = every.at[source, pl.ds(TILE, S)]
            to_depth(tail, tail, kind, step).wait_recv()

            @pl.when(source == 0)
            def _():
                head = every.at[source, pl.ds(0, TILE)]
                to_depth(head, head, kind, step, z_extra).wait_recv()

    def finish_gather(every, kind):
        for step in range(1, Z):
            tail = every.at[mz, pl.ds(TILE, S)]
            to_depth(tail, tail, kind, step).wait_send()

            @pl.when(mz == 0)
            def _():
                head = every.at[mz, pl.ds(0, TILE)]
                to_depth(head, head, kind, step, z_extra).wait_send()

    def put_together(every, dest):
        dest[0:TILE] = every[0, 0:TILE]
        for position in range(Z):
            dest[TILE + S * position : TILE + S * (position + 1)] = every[position, TILE:W]

    window = window_of(mz)
    own = (lax.broadcasted_iota(jnp.int32, (W, 1), 0) >= TILE) | (mz == 0)

    for step in range(1, E):
        to_plane(eo_send.at[0], eo_home.at[plane(step)], 4, step).wait_recv()
    mix_part[...] = nn(place[...], eo_home[...].reshape(E * CP, D)).astype(BF16)
    scatter_windows(mix_part, mix_recv, 2)
    for step in range(1, E):
        to_plane(gg_send.at[0], gg_home.at[plane(step)], 3, step).wait_recv()

    def pick_dots(e, totals):
        s0, s1 = spread(e)
        column = as_column(gg_home[e][0:1])
        return (
            totals[0] + jnp.sum(jnp.where(s0, column, 0.0), axis=0, keepdims=True),
            totals[1] + jnp.sum(jnp.where(s1, column, 0.0), axis=0, keepdims=True),
        )

    nothing = jnp.zeros((1, RP), F32)
    dots0, dots1 = lax.fori_loop(0, E, pick_dots, (nothing, nothing))
    gz_send[...] = jnp.zeros((8, RP), F32)
    gz_send[0:1] = dots0
    gz_send[1:2] = dots1
    for step in range(1, Z):
        to_depth(gz_send, gz_recv.at[mz], 3, step).start()
    gate_grad = gz_send[...]
    for step in range(1, Z):
        to_depth(gz_send, gz_recv.at[below(step)], 3, step).wait_recv()
        gate_grad = gate_grad + gz_recv[below(step)]
    both = gates[0] * gate_grad[0:1] + gates[1] * gate_grad[1:2]
    logit_grad = sum(hot[k] * (gates[k] * (gate_grad[k : k + 1] - both)) for k in range(2))
    parts = in_three(logit_grad)
    router_grad = sum(nn(p, second_low[...]) for p in parts)
    rterm[...] = sum(tn(p, router_t[...]) for p in parts)

    mixture = wait_scatter(mix_part, mix_recv, 2, mix_part[window].astype(F32))
    at = lax.broadcasted_iota(jnp.int32, (W, 1), 0) + mz * S
    bo_all[mz] = jnp.where(at < live_rows, resid[window] + mixture, 0.0).astype(BF16)
    gather_windows(bo_all, 4)

    for step in range(1, E):
        to_plane(ei_send.at[0], ei_home.at[plane(step)], 5, step).wait_recv()
    in_part[...] = nn(place[...], ei_home[...].reshape(E * CP, D)).astype(BF16)
    scatter_windows(in_part, in_recv, 5)
    cot = og[window].astype(F32)
    normal, spread_scale = normalize(resid[window])
    second_grad = wait_scatter(in_part, in_recv, 5, in_part[window].astype(F32)) + rterm[window]
    resid_grad = cot + norm_back(normal, spread_scale, second_grad * gain2[...].reshape(1, D))
    resid_win[...] = resid_grad
    ag_all[mz] = resid_grad.astype(BF16)
    gather_windows(ag_all, 6)
    sz_send[...] = jnp.zeros((8, D), F32)
    sz_send[0:1] = jnp.sum(jnp.where(own, second_grad * normal, 0.0), axis=0, keepdims=True)
    sz_send[1:2] = jnp.sum(jnp.where(own, second_grad, 0.0), axis=0, keepdims=True)
    for step in range(1, Z):
        to_depth(sz_send, sz_recv.at[mz], 7, step).start()
    wait_gather(ag_all, 6)
    put_together(ag_all, at_grad)

    mixed_grad = nt(at_grad[...], wout[...]).astype(BF16)
    grads = [[], [], []]
    for h in range(sh.heads):
        mg = mixed_grad[:, h * HEAD_DIM : (h + 1) * HEAD_DIM]
        probs = probs_s[h]
        prob_grad = nt(mg, v_s[h])
        score_grad = (
            probs * (prob_grad - jnp.sum(prob_grad * probs, axis=1, keepdims=True))
        ).astype(BF16)
        grads[0].append((nn(score_grad, k_s[h]) * scale).astype(BF16))
        grads[1].append((tn(score_grad, q_s[h]) * scale).astype(BF16))
        grads[2].append(tn(probs.astype(BF16), mg).astype(BF16))
    projected_grad = jnp.concatenate(grads[0] + grads[1] + grads[2], axis=1)
    finish_scatter(mix_part, mix_recv, 2)
    first_part = mix_part
    first_part[...] = nt(projected_grad, wqkv[...]).astype(BF16)
    scatter_windows(first_part, first_recv, 8)

    B, BP = sh.share, sh.share_rows
    qkv_grad = tn(first_low[...], projected_grad)
    for e in range(E):
        qg_send[e, 0:B] = qkv_grad[e * B : (e + 1) * B].astype(BF16)
    for step in range(1, E):
        to_plane(qg_send.at[plane(step)], qg_recv.at[me], 6, step).start()
    wout_grad = tn(at_grad[...], mixed_all[mz])
    for e in range(E):
        og_wsend[e, 0:B] = wout_grad[e * B : (e + 1) * B].astype(BF16)
    for step in range(1, E):
        to_plane(og_wsend.at[plane(step)], og_wrecv.at[me], 7, step).start()

    sums = sz_send[...]
    for step in range(1, Z):
        to_depth(sz_send, sz_recv.at[below(step)], 7, step).wait_recv()
        sums = sums + sz_recv[below(step)]
    sp_send[0:E] = router_grad
    sp_send[E : E + 4] = sums[0:4]
    for step in range(1, E):
        to_plane(sp_send, sp_recv.at[me], 8, step).start()

    normal, spread_scale = normalize(pt[window].astype(F32))
    first_grad = wait_scatter(first_part, first_recv, 8, first_part[window].astype(F32))
    patch_grad = resid_win[...] + norm_back(normal, spread_scale, first_grad * gain1[...].reshape(1, D))
    pg_all[mz] = patch_grad.astype(BF16)
    gather_windows(pg_all, 9)
    fz_send[...] = jnp.zeros((8, D), F32)
    fz_send[0:1] = jnp.sum(jnp.where(own, first_grad * normal, 0.0), axis=0, keepdims=True)
    fz_send[1:2] = jnp.sum(jnp.where(own, first_grad, 0.0), axis=0, keepdims=True)
    for step in range(1, Z):
        to_depth(fz_send, fz_recv.at[mz], 10, step).start()
    sums = fz_send[...]
    for step in range(1, Z):
        to_depth(fz_send, fz_recv.at[below(step)], 10, step).wait_recv()
        sums = sums + fz_recv[below(step)]
    fp_send[...] = sums
    for step in range(1, E):
        to_plane(fp_send, fp_recv.at[me], 9, step).start()

    wait_gather(bo_all, 4)
    put_together(bo_all, block_out)
    total = qg_send[me].astype(F32)
    total_w = og_wsend[me].astype(F32)
    total_s = sp_send[...]
    total_f = fp_send[...]
    for step in range(1, E):
        source = before(step)
        to_plane(qg_send.at[0], qg_recv.at[source], 6, step).wait_recv()
        total = total + qg_recv[source].astype(F32)
        to_plane(og_wsend.at[0], og_wrecv.at[source], 7, step).wait_recv()
        total_w = total_w + og_wrecv[source].astype(F32)
        to_plane(sp_send, sp_recv.at[source], 8, step).wait_recv()
        total_s = total_s + sp_recv[source]
        to_plane(fp_send, fp_recv.at[source], 9, step).wait_recv()
        total_f = total_f + fp_recv[source]
    qkv_out[...] = total[0:B]
    wout_out[...] = total_w[0:B]
    small_out[0:E] = total_s[0:E]
    small_out[E : E + 2] = total_s[E : E + 2]
    small_out[E + 2 : E + 4] = total_f[0:2]
    wait_gather(pg_all, 9)
    put_together(pg_all, patches_grad)

    for copy in w_out_copies + m_copies + w_passed:
        copy.wait_send()

    def sent(step, carry):
        to_plane(g_send.at[0], g_recv.at[0], 1, step).wait_send()
        to_plane(x_send.at[0], x_recv.at[0], 2, step).wait_send()
        to_plane(gg_send.at[0], gg_home.at[0], 3, step).wait_send()
        to_plane(eo_send.at[0], eo_home.at[0], 4, step).wait_send()
        to_plane(ei_send.at[0], ei_home.at[0], 5, step).wait_send()
        to_plane(qg_send.at[0], qg_recv.at[0], 6, step).wait_send()
        to_plane(og_wsend.at[0], og_wrecv.at[0], 7, step).wait_send()
        to_plane(sp_send, sp_recv.at[0], 8, step).wait_send()
        to_plane(fp_send, fp_recv.at[0], 9, step).wait_send()
        return carry

    lax.fori_loop(1, E, sent, 0)
    finish_scatter(in_part, in_recv, 5)
    finish_scatter(first_part, first_recv, 8)
    finish_gather(bo_all, 4)
    finish_gather(ag_all, 6)
    finish_gather(pg_all, 9)
    for step in range(1, Z):
        to_depth(gz_send, gz_recv.at[0], 3, step).wait_send()
        to_depth(sz_send, sz_recv.at[0], 7, step).wait_send()
        to_depth(fz_send, fz_recv.at[0], 10, step).wait_send()
    for last in (2, 1):
        strip_copy(D // strip - last, up_out, (D // strip - last) % 2).wait()
        strip_copy(F // strip - last, down_out, 2 + (F // strip - last) % 2).wait()


def scratch_of(sh, F):
    E, Z, RP, D = sh.experts, sh.depth, sh.padded, sh.width
    CP, CL, W = sh.slots, sh.slot_lanes, sh.window
    B, BP = sh.share, sh.share_rows
    L, H = sh.local, sh.heads
    blocks = (E, CP, D)

    def vm(shape, kind):
        return pltpu.VMEM(shape, kind)

    return [
        vm((D, F), BF16),
        vm((F, D), BF16),
        vm((Z, L, D), BF16),
        vm((RP, D), BF16),
        vm((RP, D), BF16),
        vm((RP, D), BF16),
        vm((H, RP, HEAD_DIM), BF16),
        vm((H, RP, HEAD_DIM), BF16),
        vm((H, RP, HEAD_DIM), BF16),
        vm((H, RP, RP), F32),
        vm((Z, RP, L), BF16),
        vm((RP, D), F32),
        vm((RP, D), BF16),
        vm((RP, E * CP), BF16),
        vm(blocks, BF16),
        vm(blocks, BF16),
        vm(blocks, BF16),
        vm(blocks, BF16),
        vm((E, 8, CL), F32),
        vm((E, 8, CL), F32),
        vm((E, CP, F), BF16),
        vm((E, CP, F), BF16),
        vm(blocks, BF16),
        vm((E, CP, F), BF16),
        vm(blocks, BF16),
        vm(blocks, BF16),
        vm(blocks, BF16),
        vm((E, 8, CL), F32),
        vm((E, 8, CL), F32),
        vm((4, 128, max(F, D)), F32),
        vm((RP, D), BF16),
        vm((Z, W, D), BF16),
        vm((RP, D), BF16),
        vm((Z, W, D), BF16),
        vm((Z, W, D), BF16),
        vm((RP, D), F32),
        vm((W, D), F32),
        vm((Z, W, D), BF16),
        vm((Z, W, D), BF16),
        vm((Z, W, D), BF16),
        vm((RP, D), BF16),
        vm((8, RP), F32),
        vm((Z, 8, RP), F32),
        vm((E, BP, 3 * L), BF16),
        vm((E, BP, 3 * L), BF16),
        vm((E, BP, L), BF16),
        vm((E, BP, L), BF16),
        vm((8, D), F32),
        vm((Z, 8, D), F32),
        vm((sh.small, D), F32),
        vm((E, sh.small, D), F32),
        vm((8, D), F32),
        vm((Z, 8, D), F32),
        vm((8, D), F32),
        vm((E, 8, D), F32),
        pltpu.SemaphoreType.DMA((4,)),
        pltpu.SemaphoreType.DMA((10, 2, E)),
        pltpu.SemaphoreType.DMA((11, 2, Z)),
        pltpu.SemaphoreType.DMA((11, 2, Z)),
        pltpu.SemaphoreType.DMA((2, Z)),
    ]


def on_device(
    mesh,
    patches,
    first_gain,
    first_bias,
    qkv_weight,
    out_weight,
    second_gain,
    second_bias,
    router_weight,
    up_weight,
    down_weight,
    expert_ids,
    router_noise,
    images_live,
    out_grad,
):
    row_count, model_width = patches.shape
    local_width = out_weight.shape[0]
    sh = Shapes(mesh, row_count, model_width, local_width)
    hidden_width = up_weight.shape[2]
    E, RP, D = sh.experts, sh.padded, sh.width
    tail = RP - row_count
    ids_row = jnp.pad(expert_ids.T, ((0, 0), (0, tail)), constant_values=-1)
    noise_row = jnp.pad(router_noise.T, ((0, 0), (0, tail)))
    vmem = pl.BlockSpec(memory_space=pltpu.VMEM)
    anywhere = pl.BlockSpec(memory_space=pl.ANY)
    slots = E * sh.slots
    flops = 2 * (
        6 * slots * D * hidden_width
        + 3 * RP * D * 4 * local_width
        + 4 * slots * RP * D
        + 7 * sh.heads * RP * RP * HEAD_DIM
    )
    outs = pl.pallas_call(
        functools.partial(whole_kernel, sh),
        out_shape=(
            jax.ShapeDtypeStruct((RP, D), BF16),
            jax.ShapeDtypeStruct((RP, D), BF16),
            jax.ShapeDtypeStruct((sh.share, 3 * local_width), F32),
            jax.ShapeDtypeStruct((sh.share, local_width), F32),
            jax.ShapeDtypeStruct((sh.small, D), F32),
            jax.ShapeDtypeStruct((D, hidden_width), F32),
            jax.ShapeDtypeStruct((hidden_width, D), F32),
        ),
        in_specs=[vmem] * 10
        + [pl.BlockSpec(memory_space=pltpu.SMEM)]
        + [vmem]
        + [anywhere] * 2,
        out_specs=(vmem,) * 5 + (anywhere,) * 2,
        scratch_shapes=scratch_of(sh, hidden_width),
        compiler_params=pltpu.CompilerParams(
            collective_id=0, has_side_effects=True, vmem_limit_bytes=62 << 20
        ),
        cost_estimate=pl.CostEstimate(flops=flops, bytes_accessed=16 << 20, transcendentals=0),
        name="block",
    )(
        patches,
        first_gain,
        first_bias,
        qkv_weight.reshape(D, 3 * local_width),
        out_weight,
        second_gain,
        second_bias,
        router_weight.T,
        ids_row,
        noise_row,
        images_live,
        out_grad,
        up_weight[0],
        down_weight[0],
    )
    block_out, patches_grad, qkv_grad, wout_grad, small, up_grad, down_grad = outs
    begin = lax.axis_index("expert") * sh.share
    mine = lax.dynamic_slice_in_dim(small, begin, sh.share, axis=1)
    return (
        block_out[:row_count],
        patches_grad[:row_count].astype(F32),
        mine[E + 2],
        mine[E + 3],
        qkv_grad.reshape(sh.share, 3, local_width),
        wout_grad.T,
        mine[E],
        mine[E + 1],
        mine[:E].T,
        up_grad[None],
        down_grad[None],
    )


def solution(mesh):
    placed = (
        P("expert", None),
        P(),
        P(),
        P(None, None, "tensor"),
        P("tensor", None),
        P(),
        P(),
        P(),
        P("expert", None, "tensor"),
        P("expert", "tensor", None),
        P("expert", None),
        P("expert", None),
        P("expert"),
        P("expert", None),
    )
    return jax.shard_map(
        functools.partial(on_device, mesh),
        mesh=mesh,
        in_specs=placed,
        out_specs=(
            P("expert", None),
            P("expert", None),
            P("expert"),
            P("expert"),
            P("expert", None, "tensor"),
            P("tensor", "expert"),
            P("expert"),
            P("expert"),
            P("expert", None),
            P("expert", None, "tensor"),
            P("expert", "tensor", None),
        ),
        check_vma=False,
    )
```

time: 676 us -> 207 us (0.31); the launches traced: 668 us -> 207 us
  blocking collectives: 305 us -> 0 us
  waiting for transfers between devices: 198 us -> 0 us
  Pallas kernels: 0 us -> 187 us
  other arithmetic: 51.8 us -> 2.18 us
  matrix products: 42.2 us -> 0 us
  local copies, waits for them, and re-layouts: 40.3 us -> 16 us
  between operations: 16.2 us -> 1.33 us
  starting transfers between devices: 13.7 us -> 0 us
    psum x1 -> x0, blocking collectives: 250 us -> none  [send_home(): summed = lax.psum(partial_sum, 'tensor').astype(jnp.bfloat16)]
    pallas_call x0 -> x1, Pallas kernels: none -> 187 us  [on_device(): pl.pallas_call(functools.partial(whole_kernel, sh), out_shape=(jax.ShapeD...]
    psum x2 -> x0, waiting for transfers between devices: 97.8 us -> none  [the longest x1 57.1 us: on_device(): lax.psum(jnp.dot(mixed, out_weight, preferred_element_type=jnp.float32),...]
    reduce_scatter x2 -> x0, waiting for transfers between devices: 50.4 us -> none  [the longest x1 45 us: on_device(): lax.psum_scatter(qkv_grad, 'expert', scatter_dimension=0, tiled=True)]
    dot_general x20 -> x0, matrix products: 40.5 us -> none  [the longest x1 6.8 us: on_device(): jnp.einsum('scd,fd->scf', delta, down_use, preferred_element_type=jnp.flo...]
    all_to_all x3 -> x0, waiting for transfers between devices: 38.1 us -> none  [the longest x1 20.9 us: send_home(): lax.all_to_all(summed, 'expert', split_axis=0, concat_axis=0, tiled=True)]
    all_to_all x1 -> x0, blocking collectives: 31.3 us -> none  [send_home(): lax.all_to_all(summed, 'expert', split_axis=0, concat_axis=0, tiled=True)]
    unnamed x1 -> x0, blocking collectives: 23.9 us -> none
  transfers between devices with their start and end apart: 8 -> 0, of which waited for: 8 -> 0; matrix products, arithmetic and copies ran while one was open for 10% -> 0% of each run, Pallas kernels for 0% -> 0%
where the time goes in v1:
time: 207 us
  Pallas kernels  187 us (90%)
  local copies, waits for them, and re-layouts  16 us (8%)
  other arithmetic  2.18 us (1%)
    pallas_call x1, Pallas kernels, on_device(): pl.pallas_call(functools.partial(whole_kernel, sh), out_shape=(jax.ShapeD...  187 us
    unnamed x11, local copies, waits for them, and re-layouts  7.26 us

profile of v1, /device:TPU:0, one launch (start us, length us, event | category | flops | bytes accessed | tf_op | source)
XLA Modules:
  0.0 206.7 jit_solution(1411564889477505287)
XLA Ops:
  0.6 2.2 %copy.28.wqkv = bf16[768,576]{1,0:T(8,128)(2,1)} copy(bf16[768,576]{0,1:T(8,128)(2,1)} %bitcast.24) | data formatting | bytes 1769472 | tf_op jit(solution)/shard_map/reshape | solution.py:836
  2.9 1.3 pad.8.ids_row
  4.2 1.3 pad.9.noise_row
  6.1 187.2 %block.1 = (bf16[400,768]{1,0:T(8,128)(2,1)}, bf16[400,768]{1,0:T(8,128)(2,1)}, f32[96,576]{1,0:T(8,128)}, f32[96,192]{1,0:T(8,128)}, f32[16,768]{1,0:T(8,128)}, /*index=5*/f32[768,768]{1,0:T(8,128)}, f32[768,768]{1,0:T(8,128)}) custom-call(bf16[394,768]{1,0:T(8,128)(2,1)} %patches.1, f32[768]{0:T(1024)} %gain1.1, f32[768]{0:T(1024)} %bias1.1, ...), custom_call_target="tpu_custom_call" | custom-call | flops 14051082240 | bytes 16777216 | tf_op jit(solution)/shard_map/block/pallas_call | solution.py:810
  193.3 0.0 copy-start.2
  193.3 0.0 copy-start.1
  193.3 1.5 dynamic-slice_bitcast_fusion.1
  194.8 1.4 dynamic-slice_bitcast_fusion
  196.2 2.2 %slice_convert_fusion = f32[394,768]{1,0:T(8,128)} fusion(bf16[400,768]{1,0:T(8,128)(2,1)} %get-tuple-element.19), kind=kLoop, calls=%fused_computation | loop fusion | flops 302592 | bytes 1815552 | tf_op jit(solution)/shard_map/convert_element_type | solution.py:853
  198.4 1.1 copy.29
  199.5 0.9 copy.30
  200.3 1.6 copy.31
  202.0 0.0 copy-done.2
  202.0 0.8 copy.36
  202.8 0.0 copy-done.1
  202.8 0.0 copy-start
  202.8 1.4 copy.37
  204.2 1.1 copy-done
  205.3 1.4 copy.38
Async XLA Ops:
  193.3 8.7 %copy-start.2 = (bf16[400,768]{1,0:T(8,128)(2,1)S(1)}, bf16[400,768]{1,0:T(8,128)(2,1)}, u32[]{:S(2)}) copy-start(bf16[400,768]{1,0:T(8,128)(2,1)} %get-tuple-element.18) | copy-start | bytes 1843204
  193.3 9.5 %copy-start.1 = (f32[768,768]{1,0:T(8,128)S(1)}, f32[768,768]{1,0:T(8,128)}, u32[]{:S(2)}) copy-start(f32[768,768]{1,0:T(8,128)} %get-tuple-element.23) | copy-start | bytes 7077892
  202.8 2.5 %copy-start = (f32[768,768]{1,0:T(8,128)S(1)}, f32[768,768]{1,0:T(8,128)}, u32[]{:S(2)}) copy-start(f32[768,768]{1,0:T(8,128)} %get-tuple-element.24) | copy-start | bytes 7077892

commit v2 on v1

v2 whole, which is shorter than its diff:
```python
import functools

import jax
import jax.numpy as jnp
from jax import lax
from jax.experimental import pallas as pl
from jax.experimental.pallas import tpu as pltpu
from jax.sharding import PartitionSpec as P

HEAD_DIM = 64
TOK_IMG = 197
TILE = 16
EPSILON = 1e-06
MESH = pl.DeviceIdType.MESH
F32 = jnp.float32
BF16 = jnp.bfloat16


def round_up(value, unit):
    return (value + unit - 1) // unit * unit


def nn(a, b):
    return lax.dot_general(a, b, (((1,), (0,)), ((), ())), preferred_element_type=F32)


def nt(a, b):
    return lax.dot_general(a, b, (((1,), (1,)), ((), ())), preferred_element_type=F32)


def tn(a, b):
    return lax.dot_general(a, b, (((0,), (0,)), ((), ())), preferred_element_type=F32)


def in_three(values):
    high = values.astype(BF16)
    rest = values - high.astype(F32)
    middle = rest.astype(BF16)
    return high, middle, (rest - middle.astype(F32)).astype(BF16)


def normalize(values):
    center = values - jnp.mean(values, axis=-1, keepdims=True)
    scale = lax.rsqrt(jnp.mean(center * center, axis=-1, keepdims=True) + EPSILON)
    return center * scale, scale


def norm_back(normal, scale, grad_normal):
    return scale * (
        grad_normal
        - jnp.mean(grad_normal, axis=-1, keepdims=True)
        - normal * jnp.mean(grad_normal * normal, axis=-1, keepdims=True)
    )


class Shapes:
    def __init__(self, mesh, row_count, model_width, local_width):
        self.experts = mesh.shape["expert"]
        self.depth = mesh.shape["tensor"]
        self.rows = row_count
        self.width = model_width
        self.local = local_width
        self.heads = local_width // HEAD_DIM
        self.padded = round_up(row_count, TILE)
        self.capacity = (3 * row_count + self.experts - 1) // self.experts
        self.slots = round_up(self.capacity, TILE)
        self.slot_lanes = round_up(self.slots, 128)
        self.step = (self.padded - TILE) // self.depth
        self.window = self.step + TILE
        self.share = model_width // self.experts
        self.share_rows = round_up(self.share, TILE)
        self.small = round_up(self.experts + 4, 8)
        self.half_rows = round_up(self.padded // 2, TILE)
        self.chunk = 256
        self.chunks = model_width // self.chunk
        parts = range(self.chunks)
        e_kinds = ["c", "g", "x", "gg", "eo", "qg", "og", "sp", "fp"] + [f"ei{c}" for c in parts]
        z_kinds = ["w", "m", "gz", "bo", "mg", "wz", "sz", "pg", "fz"]
        z_kinds += [f"{n}{c}" for n in ("mix", "in", "first") for c in parts]
        self.e_kinds = {n: i for i, n in enumerate(e_kinds)}
        self.z_kinds = {n: i for i, n in enumerate(z_kinds)}


INPUTS = (
    "gain1", "bias1", "gain2", "bias2", "router_t", "ids_row", "noise_row", "images_live", "wout",
    "out_grad", "patches", "wqkv", "up", "down",
)
OUTPUTS = (
    "block_out", "patches_grad", "qkv_out", "wout_out", "small_out", "up_out", "down_out",
)
SCRATCH = (
    "gain1", "bias1", "gain2", "bias2", "router_t", "ids_row", "noise_row", "images_live",
    "patches", "out_grad", "up", "down", "wqkv", "wfull", "pt", "og", "first_low", "q_s", "k_s",
    "v_s", "probs_s", "mixed", "mixed_all", "resid", "second_low", "place", "x_send", "x_recv",
    "c_send", "c_recv", "g_send", "g_recv", "act", "slope", "delta", "hid", "eo_send", "eo_home",
    "ei_home", "gg_send", "gg_home", "acc", "mix_part", "mix_recv", "mix_pass", "in_part",
    "in_recv", "in_pass", "first_recv", "first_pass", "rterm", "resid_win", "bo_all",
    "pg_all", "mg_send", "mg_recv", "mixed_grad", "wz_send", "wz_recv", "gz_send", "gz_recv", "qg_send", "qg_recv", "og_wsend",
    "og_wrecv", "sz_send", "sz_recv", "sp_send", "sp_recv", "fz_send", "fz_recv", "fp_send",
    "fp_recv", "qkv_sum", "wout_sum", "small_sum", "local_sem", "in_sem", "out_sem", "e_sem",
    "z_sem", "z_extra", "w_sem",
)


def whole_kernel(sh, *refs):
    E, Z, NC = sh.experts, sh.depth, sh.chunks
    R, RP, D = sh.rows, sh.padded, sh.width
    CP, CL, CW = sh.slots, sh.slot_lanes, sh.chunk
    inputs = dict(zip(INPUTS, refs))
    outputs = dict(zip(OUTPUTS, refs[len(INPUTS) :]))
    m = dict(zip(SCRATCH, refs[len(INPUTS) + len(OUTPUTS) :]))
    e_sem, z_sem, z_extra, w_sem, local_sem, in_sem, out_sem = (
        m[n] for n in ("e_sem", "z_sem", "z_extra", "w_sem", "local_sem", "in_sem", "out_sem")
    )
    me = lax.axis_index("expert")
    mz = lax.axis_index("tensor")

    def plane(step):
        return lax.rem(me + step, E)

    def before(step):
        return lax.rem(me - step + E, E)

    def above(step):
        return lax.rem(mz + step, Z)

    def below(step):
        return lax.rem(mz - step + Z, Z)

    def remote(src, dst, sems, kind, sent, received, expert, position):
        return pltpu.make_async_remote_copy(
            src_ref=src,
            dst_ref=dst,
            send_sem=sems.at[kind, 0, sent],
            recv_sem=sems.at[kind, 1, received],
            device_id=(expert, position),
            device_id_type=MESH,
        )

    def to_plane(src, dst, name, step):
        return remote(src, dst, e_sem, sh.e_kinds[name], step, step, plane(step), mz)

    def back_to(src, dst, name, step):
        return remote(src, dst, e_sem, sh.e_kinds[name], step, step, before(step), mz)

    def to_depth(src, dst, name, step, sems=None):
        sems = z_sem if sems is None else sems
        return remote(src, dst, sems, sh.z_kinds[name], step, step, me, above(step))

    relayed = Z == 4
    between = (mz > 0) & (mz < Z - 1)

    def direct(step, hold=False):
        if not relayed:
            return mz >= 0
        if step == 1:
            return mz < Z - 1
        if step == Z - 1:
            return mz > 0
        return jnp.logical_not(between) if hold else mz >= 0

    def arrives(step):
        if not relayed:
            return mz >= 0
        if step == 1:
            return mz > 0
        if step == Z - 1:
            return mz < Z - 1
        return mz >= 0

    order = (2, 1, 3) if relayed else tuple(range(1, Z))

    loads = {}
    for at, name in enumerate(INPUTS):
        dest = m["wfull"].at[mz] if name == "wout" else m[name]
        loads[name] = pltpu.make_async_copy(inputs[name], dest, in_sem.at[at])
        loads[name].start()

    def loaded(*names):
        for name in names:
            loads[name].wait()

    stores = []

    def store(src, dst, condition=None):
        copy = pltpu.make_async_copy(src, dst, out_sem.at[len(stores)])
        stores.append((copy, condition))
        if condition is None:
            copy.start()
        else:

            @pl.when(condition)
            def _():
                copy.start()

    gain1, bias1, gain2, bias2, router_t, ids_row, noise_row, images_live = (
        m[n] for n in INPUTS[:8]
    )
    barrier = pltpu.get_barrier_semaphore()
    for step in range(1, E):
        pl.semaphore_signal(barrier, inc=1, device_id=(plane(step), mz), device_id_type=MESH)
    for step in range(1, Z):
        pl.semaphore_signal(barrier, inc=1, device_id=(me, above(step)), device_id_type=MESH)

    S, W = sh.step, sh.window

    def tail_of(position):
        if isinstance(position, int):
            return pl.ds(position * S + TILE, S)
        return pl.ds(pl.multiple_of(position * S + TILE, TILE), S)

    def window_of(position):
        return pl.ds(pl.multiple_of(position * S, TILE), W)

    head, tail = pl.ds(0, TILE), pl.ds(TILE, S)

    class Scatter:
        def __init__(self, name, part, recv, passing):
            self.name, self.part, self.recv, self.passing = name, part, recv, passing

        def send_to(self, step):
            target = above(step)
            return (
                to_depth(self.part.at[tail_of(target)], self.recv.at[mz, tail], self.name, step),
                to_depth(self.part.at[head], self.recv.at[mz, head], self.name, step, z_extra),
                target == 0,
            )

        def pass_to(self):
            source = self.passing
            return (
                to_depth(source.at[tail], self.recv.at[mz, tail], self.name, 2),
                to_depth(source.at[head], self.recv.at[mz, head], self.name, 2, z_extra),
                above(2) == 0,
            )

        def far(self):
            kind = sh.z_kinds[self.name]
            up_to, down_to = (
                remote(
                    self.part.at[tail_of(Z - 1 - end)],
                    self.passing.at[tail],
                    z_sem,
                    kind,
                    0,
                    0,
                    me,
                    1 if end == 0 else Z - 2,
                )
                for end in (0, Z - 1)
            )
            down_head = remote(
                self.part.at[head],
                self.passing.at[head],
                z_extra,
                kind,
                0,
                0,
                me,
                Z - 2,
            )
            return up_to, down_to, down_head

        def start(self):
            if relayed:
                up_to, down_to, down_head = self.far()

                @pl.when(mz == 0)
                def _():
                    up_to.start()

                @pl.when(mz == Z - 1)
                def _():
                    down_to.start()
                    down_head.start()

            for step in order:
                body, first, is_head = self.send_to(step)

                @pl.when(direct(step, hold=True))
                def _():
                    body.start()

                @pl.when(direct(step, hold=True) & is_head)
                def _():
                    first.start()

        def relay(self):
            if not relayed:
                return

            @pl.when(between)
            def _():
                up_to, down_to, down_head = self.far()
                up_to.wait_recv()

                @pl.when(mz == Z - 2)
                def _():
                    down_head.wait_recv()

                target = above(2)
                self.passing[...] = (
                    self.passing[...].astype(F32) + self.part[window_of(target)].astype(F32)
                ).astype(BF16)
                body, first, is_head = self.pass_to()
                body.start()

                @pl.when(is_head)
                def _():
                    first.start()

        def total(self):
            value = self.part[window_of(mz)].astype(F32)
            for step in order:
                source = below(step)
                here = arrives(step)
                body = to_depth(
                    self.part.at[tail_of(0)], self.recv.at[source, tail], self.name, step
                )
                first = to_depth(
                    self.part.at[head], self.recv.at[source, head], self.name, step, z_extra
                )

                @pl.when(here)
                def _():
                    body.wait_recv()

                @pl.when(here & (mz == 0))
                def _():
                    first.wait_recv()

                value = value + jnp.where(here, self.recv[source].astype(F32), 0.0)
            return value

        def finish(self):
            if relayed:
                up_to, down_to, down_head = self.far()

                @pl.when(mz == 0)
                def _():
                    up_to.wait_send()

                @pl.when(mz == Z - 1)
                def _():
                    down_to.wait_send()
                    down_head.wait_send()

            for step in order:
                body, first, is_head = self.send_to(step)

                @pl.when(direct(step))
                def _():
                    body.wait_send()

                @pl.when(direct(step) & is_head)
                def _():
                    first.wait_send()

    class Gather:
        def __init__(self, name, every, body=(), first=None):
            self.name, self.every, self.body, self.first = name, every, body, first

        def copies(self, origin, step):
            block = self.every.at[(origin,) + self.body]
            found = [(to_depth(block, block, self.name, step), True)]
            if self.first is not None:
                block = self.every.at[(origin,) + self.first]
                found.append((to_depth(block, block, self.name, step, z_extra), origin == 0))
            return found

        def passed(self):
            kind, origin = sh.z_kinds[self.name], below(2)
            target, step = (Z - 1) * (mz - 1), 2 * mz - 1
            found = []
            for part, sems, holds in ((self.body, z_sem, True), (self.first, z_extra, origin == 0)):
                if part is None:
                    continue
                block = self.every.at[(origin,) + part]
                found.append(
                    (
                        remote(block, block, sems, kind, 0, step, me, target),
                        holds,
                    )
                )
            return found

        def each(self, found, condition, act):
            for copy, holds in found:

                @pl.when(condition & holds)
                def _():
                    act(copy)

        def start(self):
            for step in order:
                self.each(self.copies(mz, step), direct(step), lambda c: c.start())

        def arrival(self, step):
            self.each(self.copies(below(step), step), mz >= 0, lambda c: c.wait_recv())

        def relay(self):
            if relayed:
                self.arrival(2)
                self.each(self.passed(), between, lambda c: c.start())

        def rest(self):
            return tuple(step for step in order if not (relayed and step == 2))

        def finish(self):
            for step in order:
                self.each(self.copies(mz, step), direct(step), lambda c: c.wait_send())
            if relayed:
                self.each(self.passed(), between, lambda c: c.wait_send())

    def windows(name, every):
        return Gather(name, every, (tail,), (head,))

    def put_out(every, name, positions):
        for position in positions:
            out = outputs[name]
            store(every.at[position, tail], out.at[tail_of(position)])
            store(every.at[position, head], out.at[head], position == 0)

    def put_together(every, dest):
        dest[0:TILE] = every[0, 0:TILE]
        for position in range(Z):
            dest[TILE + S * position : TILE + S * (position + 1)] = every[position, TILE:W]

    def scatters(name, part, recv, passing):
        return [
            Scatter(f"{name}{c}", part.at[c], recv.at[c], passing.at[c]) for c in range(NC)
        ]

    window = window_of(mz)
    own = (lax.broadcasted_iota(jnp.int32, (W, 1), 0) >= TILE) | (mz == 0)

    loaded("ids_row", "images_live", "noise_row")
    live_rows = images_live[...].reshape(1, 1) * TOK_IMG
    lane = lax.broadcasted_iota(jnp.int32, (1, R), 1)
    live = (lane < live_rows).astype(F32)
    expert_of = lax.broadcasted_iota(jnp.int32, (E, R), 0)
    ids = ids_row[...]
    hot = [(expert_of == ids[k : k + 1]).astype(F32) * live for k in range(2)]
    earlier = (
        lax.broadcasted_iota(jnp.int32, (R, R), 0) < lax.broadcasted_iota(jnp.int32, (R, R), 1)
    ).astype(BF16)
    counts = [nn(h.astype(BF16), earlier) for h in hot]
    counts[1] = counts[1] + jnp.sum(hot[0], axis=1, keepdims=True)
    start = expert_of.astype(F32) * CP
    spot = [
        jnp.where(live > 0, jnp.sum(hot[k] * (counts[k] + start), axis=0, keepdims=True), -1.0)
        for k in range(2)
    ]
    blank = jnp.zeros((1, RP - R), F32)
    live, *hot = (
        jnp.concatenate([v, jnp.zeros((v.shape[0], RP - R), F32)], axis=1) for v in (live, *hot)
    )
    noise = jnp.concatenate([noise_row[...], jnp.zeros((2, RP - R), F32)], axis=1)
    spot_row = [jnp.concatenate([s, blank - 1.0], axis=1).astype(jnp.int32) for s in spot]
    eye_rows = lax.broadcasted_iota(jnp.int32, (RP, RP), 0) == lax.broadcasted_iota(
        jnp.int32, (RP, RP), 1
    )
    spot_col = [
        jnp.sum(jnp.where(eye_rows, s.astype(F32), 0.0), axis=1, keepdims=True).astype(jnp.int32)
        for s in spot_row
    ]

    def spread(e):
        slot = lax.broadcasted_iota(jnp.int32, (CP, RP), 0) + e * CP
        return slot == spot_row[0], slot == spot_row[1]

    eye_slots = lax.broadcasted_iota(jnp.int32, (CP, CL), 0) == lax.broadcasted_iota(
        jnp.int32, (CP, CL), 1
    )

    def as_row(column):
        return jnp.sum(jnp.where(eye_slots, column, 0.0), axis=0, keepdims=True)

    def as_column(row):
        return jnp.sum(jnp.where(eye_slots, row, 0.0), axis=1, keepdims=True)

    loaded("wout")
    pl.semaphore_wait(barrier, E - 1 + Z - 1)
    half = D // 2
    core = lax.rem(me, 2)
    sibling = me + 1 - 2 * core
    columns = pl.ds(pl.multiple_of(core * half, 128), half)
    weights = Gather("w", m["wfull"], (slice(None), columns))
    weights.start()

    row_of = lax.broadcasted_iota(jnp.int32, (R, 1), 0)
    og, pt = m["og"], m["pt"]
    og[pl.ds(RP - TILE, TILE)] = jnp.zeros((TILE, D), BF16)
    loaded("out_grad")
    og[0:R] = jnp.where(row_of < live_rows, m["out_grad"][...], jnp.zeros((), BF16))
    c_send, c_recv = m["c_send"], m["c_recv"]

    def pack_cotangent(step, carry):
        e = plane(step)
        s0, s1 = spread(e)
        c_send[e] = nn((s0 | s1).astype(BF16), og[...]).astype(BF16)

        @pl.when(step > 0)
        def _():
            to_plane(c_send.at[e], c_recv.at[me], "c", step).start()

        return carry

    lax.fori_loop(0, E, pack_cotangent, 0)
    c_recv[me] = c_send[me]

    pt[pl.ds(RP - TILE, TILE)] = jnp.zeros((TILE, D), BF16)
    loaded("patches", "gain1", "bias1", "gain2", "bias2", "router_t")
    pt[0:R] = m["patches"][...]
    first_low, wqkv = m["first_low"], m["wqkv"]
    g1, b1 = gain1[...].reshape(1, D), bias1[...].reshape(1, D)
    g2, b2 = gain2[...].reshape(1, D), bias2[...].reshape(1, D)
    normal, _ = normalize(pt[...].astype(F32))
    first_low[...] = (normal * g1 + b1).astype(BF16)
    loaded("wqkv")
    projected = nt(first_low[...], wqkv[...]).astype(BF16)
    q_s, k_s, v_s, probs_s = m["q_s"], m["k_s"], m["v_s"], m["probs_s"]
    for h in range(sh.heads):
        for part, dest in enumerate((q_s, k_s, v_s)):
            begin = part * sh.local + h * HEAD_DIM
            dest[h] = projected[:, begin : begin + HEAD_DIM]
    row2 = lax.broadcasted_iota(jnp.int32, (RP, RP), 0)
    col2 = lax.broadcasted_iota(jnp.int32, (RP, RP), 1)
    same = ((row2 >= TOK_IMG) == (col2 >= TOK_IMG)) & (col2 < R)
    scale = HEAD_DIM ** (-0.5)
    heads = []
    for h in range(sh.heads):
        scores = jnp.where(same, nt(q_s[h], k_s[h]) * scale, -1e30)
        exponent = jnp.exp(scores - jnp.max(scores, axis=1, keepdims=True))
        probs = exponent / jnp.sum(exponent, axis=1, keepdims=True)
        probs_s[h] = probs
        heads.append(nn(probs.astype(BF16), v_s[h]).astype(BF16))
    mixed, mixed_all = m["mixed"], m["mixed_all"]
    mixed[...] = jnp.concatenate(heads, axis=1)
    HR, L = sh.half_rows, sh.local
    mixed_all[mz] = jnp.concatenate([mixed[0:HR], mixed[RP - HR : RP]], axis=1)
    mixing = Gather("m", mixed_all)
    mixing.start()

    wfull = m["wfull"]

    def to_sibling(step):
        block = wfull.at[below(step), :, columns]
        return remote(block, block, w_sem, 0, step, step, sibling, mz)

    weights.relay()
    if relayed:
        to_sibling(2).start()
    for step in weights.rest():
        weights.arrival(step)
        to_sibling(step).start()

    resid, second_low = m["resid"], m["second_low"]

    def attend(position):
        block = mixed_all[position]
        weight = wfull[position]
        return nn(block[:, 0:L], weight), nn(block[2 * HR - RP :, L : 2 * L], weight)

    low, high = attend(mz)
    resid[0:HR] = pt[0:HR].astype(F32) + low
    resid[HR:RP] = pt[HR:RP].astype(F32) + high
    mixing.relay()
    for step in order:
        if not (relayed and step == 2):
            mixing.arrival(step)
        to_sibling(step).wait_recv()
        low, high = attend(below(step))
        resid[0:HR] += low
        resid[HR:RP] += high

    normal, _ = normalize(resid[...])
    second_low[...] = (normal * g2 + b2).astype(BF16)
    logits = nt(router_t[...], second_low[...])
    chosen = [
        jnp.sum(hot[k] * logits, axis=0, keepdims=True) + noise[k : k + 1, :] for k in range(2)
    ]
    top = jnp.maximum(chosen[0], chosen[1])
    powers = [jnp.exp(c - top) for c in chosen]
    gates = [p / (powers[0] + powers[1]) for p in powers]
    x_send, x_recv, g_send, g_recv = m["x_send"], m["x_recv"], m["g_send"], m["g_recv"]

    def pack_rows(step, carry):
        e = plane(step)
        s0, s1 = spread(e)
        x_send[e] = nn((s0 | s1).astype(BF16), second_low[...]).astype(BF16)
        gate = jnp.sum(
            jnp.where(s0, gates[0], 0.0) + jnp.where(s1, gates[1], 0.0), axis=1, keepdims=True
        )
        g_send[e] = jnp.broadcast_to(as_row(gate), (8, CL))

        @pl.when(step > 0)
        def _():
            to_plane(g_send.at[e], g_recv.at[me], "g", step).start()
            to_plane(x_send.at[e], x_recv.at[me], "x", step).start()

        return carry

    lax.fori_loop(0, E, pack_rows, 0)
    g_recv[me] = g_send[me]
    x_recv[me] = x_send[me]
    place = m["place"]
    slot_lane = lax.broadcasted_iota(jnp.int32, (RP, E * CP), 1)
    place[...] = ((slot_lane == spot_col[0]) | (slot_lane == spot_col[1])).astype(BF16)

    loaded("up", "down")
    up, down, act, slope = m["up"], m["down"], m["act"], m["slope"]
    delta, hid, eo_send, eo_home = m["delta"], m["hid"], m["eo_send"], m["eo_home"]
    gg_send, gg_home, ei_home = m["gg_send"], m["gg_home"], m["ei_home"]

    def forward(step, carry):
        group = before(step)

        @pl.when(step > 0)
        def _():
            to_plane(g_send.at[0], g_recv.at[group], "g", step).wait_recv()
            to_plane(x_send.at[0], x_recv.at[group], "x", step).wait_recv()
            to_plane(c_send.at[0], c_recv.at[group], "c", step).wait_recv()

        hidden = nn(x_recv[group], up[...])
        below_it = 0.5 * (1.0 + lax.erf(hidden * (0.5**0.5)))
        bell = jnp.exp(-0.5 * hidden * hidden) * 0.3989422804014327
        act[group] = (hidden * below_it).astype(BF16)
        slope[group] = (below_it + hidden * bell).astype(BF16)
        result = nn(act[group], down[...])
        gate = as_column(g_recv[group][0:1])
        given = c_recv[group].astype(F32)
        dots = jnp.sum(given * result, axis=1, keepdims=True)
        gg_send[group] = jnp.broadcast_to(as_row(dots), (8, CL))
        eo_send[group] = (gate * result).astype(BF16)
        delta[group] = (gate * given).astype(BF16)

        @pl.when(step > 0)
        def _():
            back_to(gg_send.at[group], gg_home.at[me], "gg", step).start()
            back_to(eo_send.at[group], eo_home.at[me], "eo", step).start()

        return carry

    lax.fori_loop(0, E, forward, 0)
    gg_home[me] = gg_send[me]
    eo_home[me] = eo_send[me]

    def cotangent_left(step, carry):
        to_plane(c_send.at[0], c_recv.at[0], "c", step).wait_send()
        return carry

    lax.fori_loop(1, E, cotangent_left, 0)
    ei_send = c_send

    def lanes(c):
        return pl.ds(c * CW, CW)

    for c in range(NC):

        def backward(step, carry):
            group = before(step)
            if c == 0:
                hid[group] = (nt(delta[group], down[...]) * slope[group]).astype(BF16)
            ei_send[group, :, lanes(c)] = nt(hid[group], up[lanes(c), :]).astype(BF16)

            @pl.when(step > 0)
            def _():
                back_to(
                    ei_send.at[group, :, lanes(c)], ei_home.at[me, :, lanes(c)], f"ei{c}", step
                ).start()

            return carry

        lax.fori_loop(0, E, backward, 0)
    ei_home[me] = ei_send[me]

    strip = 128
    F = up.shape[1]
    acc = m["acc"]

    def flat(ref, first, size):
        return ref[:, :, pl.ds(pl.multiple_of(first, 128), size)].reshape(E * CP, size)

    def strip_copy(i, out, slot):
        return pltpu.make_async_copy(
            acc.at[slot], out.at[pl.ds(pl.multiple_of(i * strip, strip), strip)], local_sem.at[slot]
        )

    def strips(out, lhs, rhs, count, slot):
        def one(i, carry):
            at = slot + lax.rem(i, 2)

            @pl.when(i >= 2)
            def _():
                strip_copy(i - 2, out, at).wait()

            acc[at] = tn(flat(lhs, i * strip, strip), flat(rhs, 0, rhs.shape[2])).astype(BF16)
            strip_copy(i, out, at).start()
            return carry

        lax.fori_loop(0, count, one, 0)

    strips(outputs["up_out"], x_recv, hid, D // strip, 0)
    strips(outputs["down_out"], act, delta, F // strip, 2)

    mix_part, in_part = m["mix_part"], m["in_part"]
    mixes = scatters("mix", mix_part, m["mix_recv"], m["mix_pass"])
    for step in range(1, E):
        to_plane(eo_send.at[0], eo_home.at[plane(step)], "eo", step).wait_recv()
    for c in range(NC):
        home = eo_home[:, :, lanes(c)].reshape(E * CP, CW)
        mix_part[c] = nn(place[...], home).astype(BF16)
        mixes[c].start()
    for step in range(1, E):
        to_plane(gg_send.at[0], gg_home.at[plane(step)], "gg", step).wait_recv()

    def pick_dots(e, totals):
        s0, s1 = spread(e)
        column = as_column(gg_home[e][0:1])
        return (
            totals[0] + jnp.sum(jnp.where(s0, column, 0.0), axis=0, keepdims=True),
            totals[1] + jnp.sum(jnp.where(s1, column, 0.0), axis=0, keepdims=True),
        )

    nothing = jnp.zeros((1, RP), F32)
    dots0, dots1 = lax.fori_loop(0, E, pick_dots, (nothing, nothing))
    gz_send, gz_recv = m["gz_send"], m["gz_recv"]
    gz_send[...] = jnp.zeros((8, RP), F32)
    gz_send[0:1] = dots0
    gz_send[1:2] = dots1
    for step in range(1, Z):
        to_depth(gz_send, gz_recv.at[mz], "gz", step).start()
    for mix in mixes:
        mix.relay()
    gate_grad = gz_send[...]
    for step in range(1, Z):
        to_depth(gz_send, gz_recv.at[below(step)], "gz", step).wait_recv()
        gate_grad = gate_grad + gz_recv[below(step)]
    both = gates[0] * gate_grad[0:1] + gates[1] * gate_grad[1:2]
    logit_grad = sum(hot[k] * (gates[k] * (gate_grad[k : k + 1] - both)) for k in range(2))
    parts = in_three(logit_grad)
    router_grad = sum(nn(p, second_low[...]) for p in parts)
    rterm = m["rterm"]
    rterm[...] = sum(tn(p, router_t[...]) for p in parts)

    ins = scatters("in", in_part, m["in_recv"], m["in_pass"])
    bo_all, pg_all = m["bo_all"], m["pg_all"]
    bo_gather = windows("bo", bo_all)
    for c in range(NC):
        for step in range(1, E):
            to_plane(
                ei_send.at[0, :, lanes(c)], ei_home.at[plane(step), :, lanes(c)], f"ei{c}", step
            ).wait_recv()
        home = ei_home[:, :, lanes(c)].reshape(E * CP, CW)
        in_part[c] = nn(place[...], home).astype(BF16)
        ins[c].start()
        if c == 0:
            mixture = jnp.concatenate([mix.total() for mix in mixes], axis=1)
            at = lax.broadcasted_iota(jnp.int32, (W, 1), 0) + mz * S
            bo_all[mz] = jnp.where(at < live_rows, resid[window] + mixture, 0.0).astype(BF16)
            bo_gather.start()
        ins[c].relay()
        if c == NC - 2:
            bo_gather.relay()

    cot = og[window].astype(F32)
    normal, spread_scale = normalize(resid[window])
    second_grad = jnp.concatenate([part.total() for part in ins], axis=1) + rterm[window]
    resid_grad = cot + norm_back(normal, spread_scale, second_grad * g2)
    resid_win = m["resid_win"]
    resid_win[...] = resid_grad
    attended_grad = jnp.where(own, resid_grad, 0.0).astype(BF16)
    mg_send, mg_recv = m["mg_send"], m["mg_recv"]

    def to_heads(step, sent, received):
        yield to_depth(mg_send.at[sent, tail], mg_recv.at[received, tail], "mg", step), mz >= 0
        first = to_depth(
            mg_send.at[sent, head], mg_recv.at[received, head], "mg", step, z_extra
        )
        yield first, received == 0

    def each(found, act):
        for copy, condition in found:

            @pl.when(condition)
            def _():
                act(copy)

    for step in order:
        mg_send[above(step)] = nt(attended_grad, wfull[above(step)]).astype(BF16)
        each(to_heads(step, above(step), mz), lambda c: c.start())
    mg_recv[mz] = nt(attended_grad, wfull[mz]).astype(BF16)
    sz_send, sz_recv = m["sz_send"], m["sz_recv"]
    sz_send[...] = jnp.zeros((8, D), F32)
    sz_send[0:1] = jnp.sum(jnp.where(own, second_grad * normal, 0.0), axis=0, keepdims=True)
    sz_send[1:2] = jnp.sum(jnp.where(own, second_grad, 0.0), axis=0, keepdims=True)
    for step in range(1, Z):
        to_depth(sz_send, sz_recv.at[mz], "sz", step).start()

    B, BP = sh.share, sh.share_rows
    qg_send, qg_recv, og_wsend, og_wrecv = (
        m[n] for n in ("qg_send", "qg_recv", "og_wsend", "og_wrecv")
    )
    lower = mz < Z // 2
    at_rows = pl.ds(pl.multiple_of(lax.rem(mz, Z // 2) * S, TILE), W)
    mixed_win = jnp.concatenate(
        [
            jnp.where(
                lower, mixed_all[p, at_rows][:, 0:L], mixed_all[p, at_rows][:, L : 2 * L]
            )
            for p in range(Z)
        ],
        axis=1,
    )
    wout_grad = tn(attended_grad, mixed_win)
    for e in range(E):
        og_wsend[e, 0:B] = wout_grad[e * B : (e + 1) * B].astype(BF16)
    for step in range(1, E):
        to_plane(og_wsend.at[plane(step)], og_wrecv.at[me], "og", step).start()
    for step in order:
        each(to_heads(step, 0, below(step)), lambda c: c.wait_recv())
    mixed_grad = m["mixed_grad"]
    put_together(mg_recv, mixed_grad)

    grads = [[], [], []]
    for h in range(sh.heads):
        mg = mixed_grad[:, h * HEAD_DIM : (h + 1) * HEAD_DIM]
        probs = probs_s[h]
        prob_grad = nt(mg, v_s[h])
        score_grad = (
            probs * (prob_grad - jnp.sum(prob_grad * probs, axis=1, keepdims=True))
        ).astype(BF16)
        grads[0].append((nn(score_grad, k_s[h]) * scale).astype(BF16))
        grads[1].append((tn(score_grad, q_s[h]) * scale).astype(BF16))
        grads[2].append(tn(probs.astype(BF16), mg).astype(BF16))
    projected_grad = jnp.concatenate(grads[0] + grads[1] + grads[2], axis=1)
    for mix in mixes:
        mix.finish()
    first_part = mix_part
    firsts = scatters("first", first_part, m["first_recv"], m["first_pass"])
    for c in range(NC):
        first_part[c] = nn(projected_grad, wqkv[:, lanes(c)]).astype(BF16)
        firsts[c].start()

    qkv_grad = tn(first_low[...], projected_grad)
    for e in range(E):
        qg_send[e, 0:B] = qkv_grad[e * B : (e + 1) * B].astype(BF16)
    for step in range(1, E):
        to_plane(qg_send.at[plane(step)], qg_recv.at[me], "qg", step).start()
    for first in firsts:
        first.relay()
    sp_send, sp_recv, fp_send, fp_recv = (m[n] for n in ("sp_send", "sp_recv", "fp_send", "fp_recv"))
    sums = sz_send[...]
    for step in range(1, Z):
        to_depth(sz_send, sz_recv.at[below(step)], "sz", step).wait_recv()
        sums = sums + sz_recv[below(step)]
    sp_send[0:E] = router_grad
    sp_send[E : E + 4] = sums[0:4]
    for step in range(1, E):
        to_plane(sp_send, sp_recv.at[me], "sp", step).start()

    for step in bo_gather.rest():
        bo_gather.arrival(step)
    put_out(bo_all, "block_out", range(Z))

    wz_send, wz_recv = m["wz_send"], m["wz_recv"]
    total_w = og_wsend[me].astype(F32)
    for step in range(1, E):
        source = before(step)
        to_plane(og_wsend.at[0], og_wrecv.at[source], "og", step).wait_recv()
        total_w = total_w + og_wrecv[source].astype(F32)
    for position in range(Z):
        wz_send[position] = total_w[:, position * L : (position + 1) * L].astype(BF16)
    for step in order:
        to_depth(wz_send.at[above(step)], wz_recv.at[mz], "wz", step).start()

    normal, spread_scale = normalize(pt[window].astype(F32))
    first_grad = jnp.concatenate([first.total() for first in firsts], axis=1)
    patch_grad = resid_win[...] + norm_back(normal, spread_scale, first_grad * g1)
    pg_all[mz] = patch_grad.astype(BF16)
    pg_gather = windows("pg", pg_all)
    fz_send, fz_recv = m["fz_send"], m["fz_recv"]
    fz_send[...] = jnp.zeros((8, D), F32)
    fz_send[0:1] = jnp.sum(jnp.where(own, first_grad * normal, 0.0), axis=0, keepdims=True)
    fz_send[1:2] = jnp.sum(jnp.where(own, first_grad, 0.0), axis=0, keepdims=True)
    for step in range(1, Z):
        to_depth(fz_send, fz_recv.at[mz], "fz", step).start()
    pg_gather.start()
    sums = fz_send[...]
    for step in range(1, Z):
        to_depth(fz_send, fz_recv.at[below(step)], "fz", step).wait_recv()
        sums = sums + fz_recv[below(step)]
    fp_send[...] = sums
    for step in range(1, E):
        to_plane(fp_send, fp_recv.at[me], "fp", step).start()

    pg_gather.relay()
    total = qg_send[me].astype(F32)
    total_s = sp_send[...]
    for step in range(1, E):
        source = before(step)
        to_plane(qg_send.at[0], qg_recv.at[source], "qg", step).wait_recv()
        total = total + qg_recv[source].astype(F32)
        to_plane(sp_send, sp_recv.at[source], "sp", step).wait_recv()
        total_s = total_s + sp_recv[source]
    qkv_sum, wout_sum, small_sum = m["qkv_sum"], m["wout_sum"], m["small_sum"]
    for part in range(3):
        qkv_sum[part] = total[0:B, part * L : (part + 1) * L]
    store(qkv_sum, outputs["qkv_out"])
    total_w = wz_send[mz].astype(F32)
    for step in order:
        to_depth(wz_send.at[0], wz_recv.at[below(step)], "wz", step).wait_recv()
        total_w = total_w + wz_recv[below(step)].astype(F32)
    wout_sum[...] = total_w[0:B]
    store(wout_sum, outputs["wout_out"])
    small_sum[...] = jnp.zeros((sh.small, D), F32)
    small_sum[0:E] = total_s[0:E]
    small_sum[E : E + 2] = total_s[E : E + 2]
    total_f = fp_send[...]
    for step in range(1, E):
        source = before(step)
        to_plane(fp_send, fp_recv.at[source], "fp", step).wait_recv()
        total_f = total_f + fp_recv[source]
    small_sum[E + 2 : E + 4] = total_f[0:2]
    store(small_sum, outputs["small_out"])

    for step in (0,) + order:
        position = below(step)
        if step and not (relayed and step == 2):
            pg_gather.arrival(step)
        put_out(pg_all, "patches_grad", [position])

    for step in range(1, Z):
        to_sibling(step).wait_send()

    def sent(step, carry):
        to_plane(g_send.at[0], g_recv.at[0], "g", step).wait_send()
        to_plane(x_send.at[0], x_recv.at[0], "x", step).wait_send()
        back_to(gg_send.at[0], gg_home.at[0], "gg", step).wait_send()
        back_to(eo_send.at[0], eo_home.at[0], "eo", step).wait_send()
        for c in range(NC):
            back_to(
                ei_send.at[0, :, lanes(c)], ei_home.at[0, :, lanes(c)], f"ei{c}", step
            ).wait_send()
        to_plane(qg_send.at[0], qg_recv.at[0], "qg", step).wait_send()
        to_plane(og_wsend.at[0], og_wrecv.at[0], "og", step).wait_send()
        to_plane(sp_send, sp_recv.at[0], "sp", step).wait_send()
        to_plane(fp_send, fp_recv.at[0], "fp", step).wait_send()
        return carry

    lax.fori_loop(1, E, sent, 0)
    for scatter in ins + firsts:
        scatter.finish()
    for gather in (weights, mixing, bo_gather, pg_gather):
        gather.finish()
    for step in range(1, Z):
        each(to_heads(step, 0, mz), lambda c: c.wait_send())
        to_depth(wz_send.at[0], wz_recv.at[0], "wz", step).wait_send()
        to_depth(gz_send, gz_recv.at[0], "gz", step).wait_send()
        to_depth(sz_send, sz_recv.at[0], "sz", step).wait_send()
        to_depth(fz_send, fz_recv.at[0], "fz", step).wait_send()
    for last in (2, 1):
        strip_copy(D // strip - last, outputs["up_out"], (D // strip - last) % 2).wait()
        strip_copy(F // strip - last, outputs["down_out"], 2 + (F // strip - last) % 2).wait()
    for copy, condition in stores:
        if condition is None:
            copy.wait()
        else:

            @pl.when(condition)
            def _():
                copy.wait()


def scratch_of(sh, F):
    E, Z, RP, R, D, NC = sh.experts, sh.depth, sh.padded, sh.rows, sh.width, sh.chunks
    CP, CL, CW, W = sh.slots, sh.slot_lanes, sh.chunk, sh.window
    B, BP = sh.share, sh.share_rows
    L, H = sh.local, sh.heads
    blocks = ((E, CP, D), BF16)
    dots = ((E, 8, CL), F32)
    rows = ((RP, D), BF16)
    part = ((NC, RP, CW), BF16)
    recv = ((NC, Z, W, CW), BF16)
    passing = ((NC, W, CW), BF16)
    every = ((Z, W, D), BF16)
    head = ((H, RP, HEAD_DIM), BF16)
    shapes = {
        "gain1": ((D,), F32),
        "bias1": ((D,), F32),
        "gain2": ((D,), F32),
        "bias2": ((D,), F32),
        "router_t": ((E, D), BF16),
        "ids_row": ((2, R), jnp.int32),
        "noise_row": ((2, R), F32),
        "images_live": ((1,), jnp.int32),
        "patches": ((R, D), BF16),
        "out_grad": ((R, D), BF16),
        "up": ((D, F), BF16),
        "down": ((F, D), BF16),
        "wqkv": ((3 * L, D), BF16),
        "wfull": ((Z, L, D), BF16),
        "pt": rows,
        "og": rows,
        "first_low": rows,
        "q_s": head,
        "k_s": head,
        "v_s": head,
        "probs_s": ((H, RP, RP), F32),
        "mixed": ((RP, L), BF16),
        "mixed_all": ((Z, sh.half_rows, 2 * L), BF16),
        "resid": ((RP, D), F32),
        "second_low": rows,
        "place": ((RP, E * CP), BF16),
        "x_send": blocks,
        "x_recv": blocks,
        "c_send": blocks,
        "c_recv": blocks,
        "g_send": dots,
        "g_recv": dots,
        "act": ((E, CP, F), BF16),
        "slope": ((E, CP, F), BF16),
        "delta": blocks,
        "hid": ((E, CP, F), BF16),
        "eo_send": blocks,
        "eo_home": blocks,
        "ei_home": blocks,
        "gg_send": dots,
        "gg_home": dots,
        "acc": ((4, 128, max(F, D)), BF16),
        "mix_part": part,
        "mix_recv": recv,
        "mix_pass": passing,
        "in_part": part,
        "in_recv": recv,
        "in_pass": passing,
        "first_recv": recv,
        "first_pass": passing,
        "rterm": ((RP, D), F32),
        "resid_win": ((W, D), F32),
        "bo_all": every,
        "pg_all": every,
        "mg_send": ((Z, W, L), BF16),
        "mg_recv": ((Z, W, L), BF16),
        "mixed_grad": ((RP, L), BF16),
        "wz_send": ((Z, BP, L), BF16),
        "wz_recv": ((Z, BP, L), BF16),
        "gz_send": ((8, RP), F32),
        "gz_recv": ((Z, 8, RP), F32),
        "qg_send": ((E, BP, 3 * L), BF16),
        "qg_recv": ((E, BP, 3 * L), BF16),
        "og_wsend": ((E, BP, Z * L), BF16),
        "og_wrecv": ((E, BP, Z * L), BF16),
        "sz_send": ((8, D), F32),
        "sz_recv": ((Z, 8, D), F32),
        "sp_send": ((sh.small, D), F32),
        "sp_recv": ((E, sh.small, D), F32),
        "fz_send": ((8, D), F32),
        "fz_recv": ((Z, 8, D), F32),
        "fp_send": ((8, D), F32),
        "fp_recv": ((E, 8, D), F32),
        "qkv_sum": ((3, B, L), F32),
        "wout_sum": ((B, L), F32),
        "small_sum": ((sh.small, D), F32),
    }
    sems = {
        "local_sem": (4,),
        "in_sem": (len(INPUTS),),
        "out_sem": (4 * Z + 3,),
        "e_sem": (len(sh.e_kinds), 2, E),
        "z_sem": (len(sh.z_kinds), 2, Z),
        "z_extra": (len(sh.z_kinds), 2, Z),
        "w_sem": (1, 2, Z),
    }
    return [
        pltpu.VMEM(*shapes[n]) if n in shapes else pltpu.SemaphoreType.DMA(sems[n]) for n in SCRATCH
    ]


def outputs_kernel(sh, pieces, *refs):
    given, outs, held, made = refs[:7], refs[7:18], refs[18:25], refs[25:36]
    in_sem, out_sem = refs[36:]
    wout, small = held[5:]
    loads = [
        pltpu.make_async_copy(src, dst, in_sem.at[at])
        for at, (src, dst) in enumerate(zip(given[5:], (wout, small)))
    ]
    steps = []
    for src, through, ready, dst, number in zip(given, held, made, outs, pieces):
        rows = src.shape[0] // number
        for piece in range(number):
            at = pl.ds(piece * rows, rows)
            part = [ref if number == 1 else ref.at[at] for ref in (src, through, ready, dst)]
            load = pltpu.make_async_copy(part[0], part[1], in_sem.at[len(loads) + len(steps)])
            steps.append((load, part))
    for load in loads + [load for load, _ in steps]:
        load.start()
    for load in loads:
        load.wait()
    E, width = sh.experts, sh.width
    begin = lax.axis_index("expert") * sh.share
    mine = pltpu.roll(small[...], lax.rem(width - begin, width), 1)[:, 0 : sh.share]
    made[5][...] = wout[...].T
    made[6][...] = mine[0:E]
    for at, gain in enumerate(made[7:]):
        gain[...] = mine[E + at]
    stores = []

    def store(src, dst):
        stores.append(pltpu.make_async_copy(src, dst, out_sem.at[len(stores)]))
        stores[-1].start()

    for src, dst in zip(made[5:], outs[5:]):
        store(src, dst)
    for load, (_, through, ready, dst) in steps:
        load.wait()
        if through.dtype == ready.dtype:
            store(through, dst)
        else:
            ready[...] = through[...].astype(ready.dtype)
            store(ready, dst)
    for copy in stores:
        copy.wait()


def on_device(
    mesh,
    patches,
    first_gain,
    first_bias,
    qkv_weight,
    out_weight,
    second_gain,
    second_bias,
    router_weight,
    up_weight,
    down_weight,
    expert_ids,
    router_noise,
    images_live,
    out_grad,
):
    row_count, model_width = patches.shape
    local_width = out_weight.shape[0]
    sh = Shapes(mesh, row_count, model_width, local_width)
    hidden_width = up_weight.shape[2]
    E, RP, D = sh.experts, sh.padded, sh.width
    anywhere = pl.BlockSpec(memory_space=pl.ANY)
    slots = E * sh.slots
    flops = 2 * (
        6 * slots * D * hidden_width
        + 3 * RP * D * 4 * local_width
        + 4 * slots * RP * D
        + 7 * sh.heads * RP * RP * HEAD_DIM
    )
    outs = pl.pallas_call(
        functools.partial(whole_kernel, sh),
        out_shape=(
            jax.ShapeDtypeStruct((RP, D), BF16),
            jax.ShapeDtypeStruct((RP, D), BF16),
            jax.ShapeDtypeStruct((3, sh.share, local_width), F32),
            jax.ShapeDtypeStruct((sh.share, local_width), F32),
            jax.ShapeDtypeStruct((sh.small, D), F32),
            jax.ShapeDtypeStruct((D, hidden_width), BF16),
            jax.ShapeDtypeStruct((hidden_width, D), BF16),
        ),
        in_specs=[anywhere] * len(INPUTS),
        out_specs=(anywhere,) * len(OUTPUTS),
        scratch_shapes=scratch_of(sh, hidden_width),
        compiler_params=pltpu.CompilerParams(
            collective_id=0, has_side_effects=True, vmem_limit_bytes=62 << 20
        ),
        cost_estimate=pl.CostEstimate(flops=flops, bytes_accessed=16 << 20, transcendentals=0),
        name="block",
    )(
        first_gain,
        first_bias,
        second_gain,
        second_bias,
        router_weight.T,
        expert_ids.T,
        router_noise.T,
        images_live,
        out_weight,
        out_grad,
        patches,
        qkv_weight.transpose(1, 2, 0).reshape(3 * local_width, D),
        up_weight[0],
        down_weight[0],
    )
    block_out, patches_grad, qkv_grad, wout_grad, small, up_grad, down_grad = outs
    pieces = (1, 1, 1, 4, 4)
    wholes = (block_out[:row_count], patches_grad[:row_count], qkv_grad, up_grad, down_grad)
    inputs = wholes + (wout_grad, small)
    kinds = (BF16, F32, F32, F32, F32)
    results = tuple(jax.ShapeDtypeStruct(w.shape, kind) for w, kind in zip(wholes, kinds)) + (
        jax.ShapeDtypeStruct((local_width, sh.share), F32),
        jax.ShapeDtypeStruct((E, sh.share), F32),
    )
    results += (jax.ShapeDtypeStruct((sh.share,), F32),) * 4
    copies = sum(pieces)
    results = pl.pallas_call(
        functools.partial(outputs_kernel, sh, pieces),
        out_shape=results,
        in_specs=[anywhere] * len(inputs),
        out_specs=(anywhere,) * len(results),
        scratch_shapes=[pltpu.VMEM(w.shape, w.dtype) for w in inputs + results]
        + [pltpu.SemaphoreType.DMA((copies + 2,)), pltpu.SemaphoreType.DMA((copies + 6,))],
        compiler_params=pltpu.CompilerParams(vmem_limit_bytes=62 << 20),
        name="outputs",
    )(*inputs)
    block_out, patches_grad, qkv_grad, up_grad, down_grad, wout_grad, router_grad = results[:7]
    gain2_grad, bias2_grad, gain1_grad, bias1_grad = results[7:]
    return (
        block_out,
        patches_grad,
        gain1_grad,
        bias1_grad,
        qkv_grad.transpose(1, 0, 2),
        wout_grad,
        gain2_grad,
        bias2_grad,
        router_grad.T,
        up_grad[None],
        down_grad[None],
    )


def solution(mesh):
    placed = (
        P("expert", None),
        P(),
        P(),
        P(None, None, "tensor"),
        P("tensor", None),
        P(),
        P(),
        P(),
        P("expert", None, "tensor"),
        P("expert", "tensor", None),
        P("expert", None),
        P("expert", None),
        P("expert"),
        P("expert", None),
    )
    return jax.shard_map(
        functools.partial(on_device, mesh),
        mesh=mesh,
        in_specs=placed,
        out_specs=(
            P("expert", None),
            P("expert", None),
            P("expert"),
            P("expert"),
            P("expert", None, "tensor"),
            P("tensor", "expert"),
            P("expert"),
            P("expert"),
            P("expert", None),
            P("expert", None, "tensor"),
            P("expert", "tensor", None),
        ),
        check_vma=False,
    )
```

time: 207 us -> 158 us (0.76)
  Pallas kernels: 187 us -> 157 us
  local copies, waits for them, and re-layouts: 16 us -> 0 us
  other arithmetic: 2.18 us -> 0 us
    pallas_call x1, Pallas kernels: 187 us -> 152 us  [on_device(): pl.pallas_call(functools.partial(whole_kernel, sh), out_shape=(jax.ShapeD...]
    unnamed x11 -> x0, local copies, waits for them, and re-layouts: 7.26 us -> none
    pallas_call x0 -> x1, Pallas kernels: none -> 4.32 us  [on_device(): pl.pallas_call(functools.partial(outputs_kernel, sh, pieces), out_shape=r...]
    pad x2 -> x0, local copies, waits for them, and re-layouts: 2.57 us -> none  [the longest x1 1.28 us: on_device(): ids_row = jnp.pad(expert_ids.T, ((0, 0), (0, tail)), constant_values=-1)]
    reshape x1 -> x0, local copies, waits for them, and re-layouts: 2.22 us -> none  [on_device(): qkv_weight.reshape(D, 3 * local_width)]
    convert_element_type x1 -> x0, other arithmetic: 2.18 us -> none  [on_device(): patches_grad[:row_count].astype(F32)]
where the time goes in v2:
time: 158 us
  Pallas kernels  157 us (99%)
    pallas_call x1, Pallas kernels, on_device(): pl.pallas_call(functools.partial(whole_kernel, sh), out_shape=(jax.ShapeD...  152 us
    pallas_call x1, Pallas kernels, on_device(): pl.pallas_call(functools.partial(outputs_kernel, sh, pieces), out_shape=r...  4.32 us

profile of v2, /device:TPU:0, one launch (start us, length us, event | category | flops | bytes accessed | tf_op | source)
XLA Modules:
  0.0 158.0 jit_solution(891159526592422856)
XLA Ops:
  1.3 152.2 %block.1 = (bf16[400,768]{1,0:T(8,128)(2,1)}, bf16[400,768]{1,0:T(8,128)(2,1)}, f32[3,96,192]{2,1,0:T(8,128)}, f32[96,192]{1,0:T(8,128)}, f32[16,768]{1,0:T(8,12...) custom-call(f32[768]{0:T(1024)} %refs_0_.1, f32[768]{0:T(1024)} %refs_1_.1, f32[768]{0:T(1024)} %refs_2_.1, ...), custom_call_target="tpu_custom_call" | custom-call | flops 14051082240 | bytes 16777216 | tf_op jit(solution)/shard_map/block/pallas_call | solution.py:1157
  153.5 4.3 %outputs.1 = (bf16[394,768]{1,0:T(8,128)(2,1)}, f32[394,768]{1,0:T(8,128)}, f32[3,96,192]{2,1,0:T(8,128)}, f32[768,768]{1,0:T(8,128)}, f32[768,768]{1,0:T(8,128)...) custom-call(bf16[394,768]{1,0:T(8,128)(2,1)} %bitcast.14, ...), custom_call_target="tpu_custom_call" | custom-call | tf_op jit(solution)/shard_map/outputs/pallas_call | solution.py:1203

commit v3 on v2

v3 whole, which is shorter than its diff:
```python
import functools
from types import SimpleNamespace

import jax
import jax.numpy as jnp
from jax import lax
from jax.experimental import pallas as pl
from jax.experimental.pallas import tpu as pltpu
from jax.sharding import PartitionSpec as P

HEAD_DIM = 64
TOK_IMG = 197
TILE = 16
EPSILON = 1e-06
MESH = pl.DeviceIdType.MESH
F32 = jnp.float32
BF16 = jnp.bfloat16


def round_up(value, unit):
    return (value + unit - 1) // unit * unit


def nn(a, b):
    return lax.dot_general(a, b, (((1,), (0,)), ((), ())), preferred_element_type=F32)


def nt(a, b):
    return lax.dot_general(a, b, (((1,), (1,)), ((), ())), preferred_element_type=F32)


def tn(a, b):
    return lax.dot_general(a, b, (((0,), (0,)), ((), ())), preferred_element_type=F32)


def in_three(values):
    high = values.astype(BF16)
    rest = values - high.astype(F32)
    middle = rest.astype(BF16)
    return high, middle, (rest - middle.astype(F32)).astype(BF16)


def normalize(values):
    center = values - jnp.mean(values, axis=-1, keepdims=True)
    scale = lax.rsqrt(jnp.mean(center * center, axis=-1, keepdims=True) + EPSILON)
    return center * scale, scale


def norm_back(normal, scale, grad_normal):
    return scale * (
        grad_normal
        - jnp.mean(grad_normal, axis=-1, keepdims=True)
        - normal * jnp.mean(grad_normal * normal, axis=-1, keepdims=True)
    )


class Shapes:
    def __init__(self, mesh, row_count, model_width, local_width):
        self.experts = mesh.shape["expert"]
        self.depth = mesh.shape["tensor"]
        self.rows = row_count
        self.width = model_width
        self.local = local_width
        self.heads = local_width // HEAD_DIM
        self.padded = round_up(row_count, TILE)
        self.capacity = (3 * row_count + self.experts - 1) // self.experts
        self.slots = round_up(self.capacity, TILE)
        self.split = self.depth * TILE if self.slots >= 2 * self.depth * TILE else 0
        self.common = self.slots - self.split
        self.slot_lanes = round_up(self.slots, 128)
        self.step = (self.padded - TILE) // self.depth
        self.window = self.step + TILE
        self.share = model_width // self.experts
        self.share_rows = round_up(self.share, TILE)
        self.small = round_up(self.experts + 4, 8)
        self.near_lanes = min(256, model_width)
        self.half_rows = round_up(self.padded // 2, TILE)
        self.chunk = 256
        self.chunks = model_width // self.chunk
        (
            self.e_c,
            self.e_g,
            self.e_x,
            self.e_gg,
            self.e_eo,
            self.e_xs,
            self.e_ei,
        ) = range(7)
        self.e_kinds = self.e_ei + self.chunks
        self.chips = self.experts // 2
        self.s_w, self.s_qg, self.s_og, self.s_sp = range(4)
        self.s_kinds = 4
        (
            self.z_w,
            self.z_m,
            self.z_gz,
            self.z_bo,
            self.z_mg,
            self.z_wz,
            self.z_pg,
            self.z_zs,
            self.z_mix,
            self.z_first,
            self.z_x,
        ) = range(11)
        self.z_in = self.z_x + 2
        self.z_kinds = self.z_in + self.chunks


    def near(self, expert):
        return jnp.minimum(expert * self.share // 128 * 128, self.width - self.near_lanes)


def whole_kernel(sh, fields, *refs):
    E, Z, NC = sh.experts, sh.depth, sh.chunks
    R, RP, D = sh.rows, sh.padded, sh.width
    CP, CL, CW = sh.slots, sh.slot_lanes, sh.chunk
    taken = iter(refs)
    inputs, outputs, m = (SimpleNamespace(**{f: next(taken) for f in group}) for group in fields)
    e_sem, z_sem, z_extra, s_sem, c_sem = m.e_sem, m.z_sem, m.z_extra, m.s_sem, m.c_sem
    local_sem, in_sem, out_sem = m.local_sem, m.in_sem, m.out_sem
    me = lax.axis_index("expert")
    mz = lax.axis_index("tensor")

    def plane(step):
        return lax.rem(me + step, E)

    def before(step):
        return lax.rem(me - step + E, E)

    def above(step):
        return lax.rem(mz + step, Z)

    def below(step):
        return lax.rem(mz - step + Z, Z)

    def remote(src, dst, sems, kind, sent, received, expert, position):
        return pltpu.make_async_remote_copy(
            src_ref=src,
            dst_ref=dst,
            send_sem=sems.at[kind, 0, sent],
            recv_sem=sems.at[kind, 1, received],
            device_id=(expert, position),
            device_id_type=MESH,
        )

    def to_plane(src, dst, kind, step):
        return remote(src, dst, e_sem, kind, step, step, plane(step), mz)

    core = lax.rem(me, 2)
    chip = me // 2
    sibling = me + 1 - 2 * core

    def to_sibling(src, dst, kind, step=0):
        return remote(src, dst, s_sem, kind, step, step, sibling, mz)

    def to_chip(src, dst, kind, step):
        target = lax.rem(chip + step, sh.chips)
        return remote(src, dst, c_sem, kind, step, step, 2 * target + core, mz)

    def chip_after(step):
        return lax.rem(chip + step, sh.chips)

    def chip_before(step):
        return lax.rem(chip - step + sh.chips, sh.chips)

    class ChipSum:
        def __init__(self, kind, send, pair, recv):
            self.kind, self.send, self.pair, self.recv = kind, send, pair, recv

        def halves(self):
            return to_sibling(self.send.at[1 - core], self.pair, self.kind)

        def start(self):
            self.halves().start()

        def cross(self):
            self.halves().wait_recv()
            half = self.send[core].astype(F32) + self.pair[...].astype(F32)
            self.send[core] = half.astype(self.send.dtype)
            for step in range(1, sh.chips):
                self.block(step, chip_after(step)).start()

        def block(self, step, target):
            return to_chip(self.send.at[core, target], self.recv.at[chip], self.kind, step)

        def total(self):
            value = self.send[core, chip].astype(F32)
            for step in range(1, sh.chips):
                source = chip_before(step)
                to_chip(
                    self.send.at[core, 0], self.recv.at[source], self.kind, step
                ).wait_recv()
                value = value + self.recv[source].astype(F32)
            return value

        def finish(self):
            self.halves().wait_send()
            for step in range(1, sh.chips):
                self.block(step, 0).wait_send()

    class SmallSum:
        def __init__(self, kind, send, pair, half, recv):
            self.kind, self.send, self.pair, self.half, self.recv = kind, send, pair, half, recv

        def exchange(self):
            return to_sibling(self.send, self.pair, self.kind)

        def start(self):
            self.exchange().start()

        def cross(self):
            self.exchange().wait_recv()
            self.half[...] = self.send[...] + self.pair[...]
            for step in range(1, sh.chips):
                to_chip(self.half, self.recv.at[chip], self.kind, step).start()

        def total(self):
            value = self.half[...]
            for step in range(1, sh.chips):
                source = chip_before(step)
                to_chip(self.half, self.recv.at[source], self.kind, step).wait_recv()
                value = value + self.recv[source]
            return value

        def finish(self):
            self.exchange().wait_send()
            for step in range(1, sh.chips):
                to_chip(self.half, self.recv.at[chip], self.kind, step).wait_send()

    def back_to(src, dst, kind, step):
        return remote(src, dst, e_sem, kind, step, step, before(step), mz)

    def to_depth(src, dst, kind, step, sems=None):
        sems = z_sem if sems is None else sems
        return remote(src, dst, sems, kind, step, step, me, above(step))

    relayed = Z == 4
    between = (mz > 0) & (mz < Z - 1)

    def direct(step, hold=False):
        if not relayed:
            return mz >= 0
        if step == 1:
            return mz < Z - 1
        if step == Z - 1:
            return mz > 0
        return jnp.logical_not(between) if hold else mz >= 0

    def arrives(step):
        if not relayed:
            return mz >= 0
        if step == 1:
            return mz > 0
        if step == Z - 1:
            return mz < Z - 1
        return mz >= 0

    order = (2, 1, 3) if relayed else tuple(range(1, Z))

    m.wout = m.wfull.at[mz]
    loads = SimpleNamespace()
    for at, (field, source) in enumerate(vars(inputs).items()):
        copy = pltpu.make_async_copy(source, getattr(m, field), in_sem.at[at])
        copy.start()
        setattr(loads, field, copy)

    def loaded(*copies):
        for copy in copies:
            copy.wait()

    stores = []

    def store(src, dst, condition=None):
        copy = pltpu.make_async_copy(src, dst, out_sem.at[len(stores)])
        stores.append((copy, condition))
        if condition is None:
            copy.start()
        else:

            @pl.when(condition)
            def _():
                copy.start()

    gain1, bias1, gain2, bias2 = m.gain1, m.bias1, m.gain2, m.bias2
    router_t, ids_row, noise_row, images_live = m.router_t, m.ids_row, m.noise_row, m.images_live
    barrier = pltpu.get_barrier_semaphore()
    for step in range(1, E):
        pl.semaphore_signal(barrier, inc=1, device_id=(plane(step), mz), device_id_type=MESH)
    for step in range(1, Z):
        pl.semaphore_signal(barrier, inc=1, device_id=(me, above(step)), device_id_type=MESH)

    S, W = sh.step, sh.window

    def tail_of(position):
        if isinstance(position, int):
            return pl.ds(position * S + TILE, S)
        return pl.ds(pl.multiple_of(position * S + TILE, TILE), S)

    def window_of(position):
        return pl.ds(pl.multiple_of(position * S, TILE), W)

    head, tail = pl.ds(0, TILE), pl.ds(TILE, S)

    class Scatter:
        def __init__(self, kind, part, recv, passing):
            self.kind, self.part, self.recv, self.passing = kind, part, recv, passing

        def send_to(self, step):
            target = above(step)
            return (
                to_depth(self.part.at[tail_of(target)], self.recv.at[mz, tail], self.kind, step),
                to_depth(self.part.at[head], self.recv.at[mz, head], self.kind, step, z_extra),
                target == 0,
            )

        def pass_to(self):
            source = self.passing
            return (
                to_depth(source.at[tail], self.recv.at[mz, tail], self.kind, 2),
                to_depth(source.at[head], self.recv.at[mz, head], self.kind, 2, z_extra),
                above(2) == 0,
            )

        def far(self):
            kind = self.kind
            up_to, down_to = (
                remote(
                    self.part.at[tail_of(Z - 1 - end)],
                    self.passing.at[tail],
                    z_sem,
                    kind,
                    0,
                    0,
                    me,
                    1 if end == 0 else Z - 2,
                )
                for end in (0, Z - 1)
            )
            down_head = remote(
                self.part.at[head],
                self.passing.at[head],
                z_extra,
                kind,
                0,
                0,
                me,
                Z - 2,
            )
            return up_to, down_to, down_head

        def start(self):
            if relayed:
                up_to, down_to, down_head = self.far()

                @pl.when(mz == 0)
                def _():
                    up_to.start()

                @pl.when(mz == Z - 1)
                def _():
                    down_to.start()
                    down_head.start()

            for step in order:
                body, first, is_head = self.send_to(step)

                @pl.when(direct(step, hold=True))
                def _():
                    body.start()

                @pl.when(direct(step, hold=True) & is_head)
                def _():
                    first.start()

        def relay(self):
            if not relayed:
                return

            @pl.when(between)
            def _():
                up_to, down_to, down_head = self.far()
                up_to.wait_recv()

                @pl.when(mz == Z - 2)
                def _():
                    down_head.wait_recv()

                target = above(2)
                self.passing[...] = (
                    self.passing[...].astype(F32) + self.part[window_of(target)].astype(F32)
                ).astype(BF16)
                body, first, is_head = self.pass_to()
                body.start()

                @pl.when(is_head)
                def _():
                    first.start()

        def total(self):
            value = self.part[window_of(mz)].astype(F32)
            for step in order:
                source = below(step)
                here = arrives(step)
                body = to_depth(
                    self.part.at[tail_of(0)], self.recv.at[source, tail], self.kind, step
                )
                first = to_depth(
                    self.part.at[head], self.recv.at[source, head], self.kind, step, z_extra
                )

                @pl.when(here)
                def _():
                    body.wait_recv()

                @pl.when(here & (mz == 0))
                def _():
                    first.wait_recv()

                value = value + jnp.where(here, self.recv[source].astype(F32), 0.0)
            return value

        def finish(self):
            if relayed:
                up_to, down_to, down_head = self.far()

                @pl.when(mz == 0)
                def _():
                    up_to.wait_send()

                @pl.when(mz == Z - 1)
                def _():
                    down_to.wait_send()
                    down_head.wait_send()

            for step in order:
                body, first, is_head = self.send_to(step)

                @pl.when(direct(step))
                def _():
                    body.wait_send()

                @pl.when(direct(step) & is_head)
                def _():
                    first.wait_send()

    class Gather:
        def __init__(self, kind, every, body=(), first=None):
            self.kind, self.every, self.body, self.first = kind, every, body, first

        def blocks(self, origin):
            found = [(self.every.at[(origin,) + self.body], z_sem, True)]
            if self.first is not None:
                found.append((self.every.at[(origin,) + self.first], z_extra, origin == 0))
            return found

        def copies(self, origin, step):
            return [
                (to_depth(block, block, self.kind, step, sems), holds)
                for block, sems, holds in self.blocks(origin)
            ]

        def passed(self):
            target, step = (Z - 1) * (mz - 1), 2 * mz - 1
            return [
                (remote(block, block, sems, self.kind, 0, step, me, target), holds)
                for block, sems, holds in self.blocks(below(2))
            ]

        def each(self, found, condition, act):
            for copy, holds in found:

                @pl.when(condition & holds)
                def _():
                    act(copy)

        def start(self):
            for step in order:
                self.each(self.copies(mz, step), direct(step), lambda c: c.start())

        def arrival(self, step):
            self.each(self.copies(below(step), step), mz >= 0, lambda c: c.wait_recv())

        def relay(self):
            if relayed:
                self.arrival(2)
                self.each(self.passed(), between, lambda c: c.start())

        def rest(self):
            return tuple(step for step in order if not (relayed and step == 2))

        def finish(self):
            for step in order:
                self.each(self.copies(mz, step), direct(step), lambda c: c.wait_send())
            if relayed:
                self.each(self.passed(), between, lambda c: c.wait_send())

    def split_rows(position):
        return pl.ds(pl.multiple_of(sh.common + position * TILE, TILE), TILE)

    class Strips(Gather):
        def blocks(self, origin):
            return [(self.every.at[self.body, split_rows(origin)], z_sem, True)]

    def windows(kind, every):
        return Gather(kind, every, (tail,), (head,))

    def put_out(every, out, positions):
        for position in positions:
            store(every.at[position, tail], out.at[tail_of(position)])
            store(every.at[position, head], out.at[head], position == 0)

    def put_together(every, dest):
        dest[0:TILE] = every[0, 0:TILE]
        for position in range(Z):
            dest[TILE + S * position : TILE + S * (position + 1)] = every[position, TILE:W]

    def scatters(kind, part, recv, passing):
        return [
            Scatter(kind + c, part.at[c], recv.at[c], passing.at[c]) for c in range(NC)
        ]

    window = window_of(mz)
    own = (lax.broadcasted_iota(jnp.int32, (W, 1), 0) >= TILE) | (mz == 0)

    loaded(loads.ids_row, loads.images_live, loads.noise_row)
    live_rows = images_live[...].reshape(1, 1) * TOK_IMG
    lane = lax.broadcasted_iota(jnp.int32, (1, R), 1)
    live = (lane < live_rows).astype(F32)
    expert_of = lax.broadcasted_iota(jnp.int32, (E, R), 0)
    ids = ids_row[...]
    hot = [(expert_of == ids[k : k + 1]).astype(F32) * live for k in range(2)]
    earlier = (
        lax.broadcasted_iota(jnp.int32, (R, R), 0) < lax.broadcasted_iota(jnp.int32, (R, R), 1)
    ).astype(BF16)
    counts = [nn(h.astype(BF16), earlier) for h in hot]
    counts[1] = counts[1] + jnp.sum(hot[0], axis=1, keepdims=True)
    start = expert_of.astype(F32) * CP
    spot = [
        jnp.where(live > 0, jnp.sum(hot[k] * (counts[k] + start), axis=0, keepdims=True), -1.0)
        for k in range(2)
    ]
    blank = jnp.zeros((1, RP - R), F32)
    live, *hot = (
        jnp.concatenate([v, jnp.zeros((v.shape[0], RP - R), F32)], axis=1) for v in (live, *hot)
    )
    noise = jnp.concatenate([noise_row[...], jnp.zeros((2, RP - R), F32)], axis=1)
    spot_row = [jnp.concatenate([s, blank - 1.0], axis=1).astype(jnp.int32) for s in spot]
    eye_rows = lax.broadcasted_iota(jnp.int32, (RP, RP), 0) == lax.broadcasted_iota(
        jnp.int32, (RP, RP), 1
    )
    spot_col = [
        jnp.sum(jnp.where(eye_rows, s.astype(F32), 0.0), axis=1, keepdims=True).astype(jnp.int32)
        for s in spot_row
    ]

    def spread(e):
        slot = lax.broadcasted_iota(jnp.int32, (CP, RP), 0) + e * CP
        return slot == spot_row[0], slot == spot_row[1]

    eye_slots = lax.broadcasted_iota(jnp.int32, (CP, CL), 0) == lax.broadcasted_iota(
        jnp.int32, (CP, CL), 1
    )

    def as_row(column):
        return jnp.sum(jnp.where(eye_slots, column, 0.0), axis=0, keepdims=True)

    def as_column(row):
        return jnp.sum(jnp.where(eye_slots, row, 0.0), axis=1, keepdims=True)

    loaded(loads.wout)
    pl.semaphore_wait(barrier, E - 1 + Z - 1)
    half = D // 2
    columns = pl.ds(pl.multiple_of(core * half, 128), half)
    weights = Gather(sh.z_w, m.wfull, (slice(None), columns))
    weights.start()

    row_of = lax.broadcasted_iota(jnp.int32, (R, 1), 0)
    og, pt = m.og, m.pt
    og[pl.ds(RP - TILE, TILE)] = jnp.zeros((TILE, D), BF16)
    loaded(loads.out_grad)
    og[0:R] = jnp.where(row_of < live_rows, m.out_grad[...], jnp.zeros((), BF16))
    c_send, c_recv = m.c_send, m.c_recv

    def pack_cotangent(step, carry):
        e = plane(step)
        s0, s1 = spread(e)
        c_send[e] = nn((s0 | s1).astype(BF16), og[...]).astype(BF16)

        @pl.when(step > 0)
        def _():
            to_plane(c_send.at[e], c_recv.at[step], sh.e_c, step).start()

        return carry

    lax.fori_loop(0, E, pack_cotangent, 0)
    c_recv[0] = c_send[me]

    pt[pl.ds(RP - TILE, TILE)] = jnp.zeros((TILE, D), BF16)
    loaded(loads.patches, loads.gain1, loads.bias1, loads.gain2, loads.bias2, loads.router_t)
    pt[0:R] = m.patches[...]
    first_low, wqkv = m.first_low, m.wqkv
    g1, b1 = gain1[...].reshape(1, D), bias1[...].reshape(1, D)
    g2, b2 = gain2[...].reshape(1, D), bias2[...].reshape(1, D)
    normal, _ = normalize(pt[...].astype(F32))
    first_low[...] = (normal * g1 + b1).astype(BF16)
    loaded(loads.wqkv)
    projected = nt(first_low[...], wqkv[...]).astype(BF16)
    q_s, k_s, v_s, probs_s = m.q_s, m.k_s, m.v_s, m.probs_s
    for h in range(sh.heads):
        for part, dest in enumerate((q_s, k_s, v_s)):
            begin = part * sh.local + h * HEAD_DIM
            dest[h] = projected[:, begin : begin + HEAD_DIM]
    row2 = lax.broadcasted_iota(jnp.int32, (RP, RP), 0)
    col2 = lax.broadcasted_iota(jnp.int32, (RP, RP), 1)
    same = ((row2 >= TOK_IMG) == (col2 >= TOK_IMG)) & (col2 < R)
    scale = HEAD_DIM ** (-0.5)
    heads = []
    for h in range(sh.heads):
        scores = jnp.where(same, nt(q_s[h], k_s[h]) * scale, -1e30)
        exponent = jnp.exp(scores - jnp.max(scores, axis=1, keepdims=True))
        probs = exponent / jnp.sum(exponent, axis=1, keepdims=True)
        probs_s[h] = probs
        heads.append(nn(probs.astype(BF16), v_s[h]).astype(BF16))
    mixed, mixed_all = m.mixed, m.mixed_all
    mixed[...] = jnp.concatenate(heads, axis=1)
    HR, L = sh.half_rows, sh.local
    mixed_all[mz] = jnp.concatenate([mixed[0:HR], mixed[RP - HR : RP]], axis=1)
    mixing = Gather(sh.z_m, mixed_all)
    mixing.start()

    wfull = m.wfull

    def to_other(step):
        block = wfull.at[below(step), :, columns]
        return to_sibling(block, block, sh.s_w, step)

    weights.relay()
    if relayed:
        to_other(2).start()
    for step in weights.rest():
        weights.arrival(step)
        to_other(step).start()

    resid, second_low = m.resid, m.second_low

    def attend(position):
        block = mixed_all[position]
        weight = wfull[position]
        return nn(block[:, 0:L], weight), nn(block[2 * HR - RP :, L : 2 * L], weight)

    low, high = attend(mz)
    resid[0:HR] = pt[0:HR].astype(F32) + low
    resid[HR:RP] = pt[HR:RP].astype(F32) + high
    mixing.relay()
    for step in order:
        if not (relayed and step == 2):
            mixing.arrival(step)
        to_other(step).wait_recv()
        low, high = attend(below(step))
        resid[0:HR] += low
        resid[HR:RP] += high

    normal, _ = normalize(resid[...])
    second_low[...] = (normal * g2 + b2).astype(BF16)
    logits = nt(router_t[...], second_low[...])
    chosen = [
        jnp.sum(hot[k] * logits, axis=0, keepdims=True) + noise[k : k + 1, :] for k in range(2)
    ]
    top = jnp.maximum(chosen[0], chosen[1])
    powers = [jnp.exp(c - top) for c in chosen]
    gates = [p / (powers[0] + powers[1]) for p in powers]
    x_send, x_recv, g_send, g_recv = m.x_send, m.x_recv, m.g_send, m.g_recv

    def pack_rows(step, carry):
        e = plane(step)
        s0, s1 = spread(e)
        x_send[e] = nn((s0 | s1).astype(BF16), second_low[...]).astype(BF16)
        gate = jnp.sum(
            jnp.where(s0, gates[0], 0.0) + jnp.where(s1, gates[1], 0.0), axis=1, keepdims=True
        )
        g_send[e] = jnp.broadcast_to(as_row(gate), (8, CL))

        @pl.when(step > 0)
        def _():
            to_plane(g_send.at[e], g_recv.at[step], sh.e_g, step).start()
            if sh.split:
                strip_to(e, step).start()
            else:
                common_to(e, step).start()

        return carry

    common = pl.ds(0, sh.common)

    def common_to(sent, step):
        return to_plane(x_send.at[sent, common], x_recv.at[step, common], sh.e_x, step)

    def strip_to(sent, step):
        rows = split_rows(mz)
        return to_plane(x_send.at[sent, rows], x_recv.at[step, rows], sh.e_xs, step)

    lax.fori_loop(0, E, pack_rows, 0)
    if sh.split:

        def send_common(step, carry):
            common_to(plane(step), step).start()
            return carry

        lax.fori_loop(1, E, send_common, 0)
        x_recv[0, split_rows(mz)] = x_send[me, split_rows(mz)]
    g_recv[0] = g_send[me]
    x_recv[0, common] = x_send[me, common]
    place = m.place
    slot_lane = lax.broadcasted_iota(jnp.int32, (RP, E * CP), 1)
    place[...] = ((slot_lane == spot_col[0]) | (slot_lane == spot_col[1])).astype(BF16)

    loaded(loads.up, loads.down)
    up, down, act, slope = m.up, m.down, m.act, m.slope
    delta, hid, eo_send, eo_home = m.delta, m.hid, m.eo_send, m.eo_home
    gg_send, gg_home, ei_home = m.gg_send, m.gg_home, m.ei_home

    halves = ((0, E // 2), (E // 2, E))
    x_strips = [Strips(sh.z_x + at, x_recv, pl.ds(a, b - a)) for at, (a, b) in enumerate(halves)]
    if sh.split:

        def strip_arrived(step, carry):
            strip_to(0, step).wait_recv()
            return carry

        for strips_of, (a, b) in zip(x_strips, halves):
            lax.fori_loop(max(a, 1), b, strip_arrived, 0)
            strips_of.start()

    def forward(step, carry):

        @pl.when(step > 0)
        def _():
            to_plane(g_send.at[0], g_recv.at[step], sh.e_g, step).wait_recv()
            common_to(0, step).wait_recv()
            to_plane(c_send.at[0], c_recv.at[step], sh.e_c, step).wait_recv()

        hidden = nn(x_recv[step], up[...])
        below_it = 0.5 * (1.0 + lax.erf(hidden * (0.5**0.5)))
        bell = jnp.exp(-0.5 * hidden * hidden) * 0.3989422804014327
        act[step] = (hidden * below_it).astype(BF16)
        slope[step] = (below_it + hidden * bell).astype(BF16)
        result = nn(act[step], down[...])
        gate = as_column(g_recv[step][0:1])
        given = c_recv[step].astype(F32)
        dots = jnp.sum(given * result, axis=1, keepdims=True)
        gg_send[step] = jnp.broadcast_to(as_row(dots), (8, CL))
        eo_send[step] = (gate * result).astype(BF16)
        delta[step] = (gate * given).astype(BF16)

        @pl.when(step > 0)
        def _():
            back_to(gg_send.at[step], gg_home.at[me], sh.e_gg, step).start()
            back_to(eo_send.at[step], eo_home.at[me], sh.e_eo, step).start()

        return carry

    for strips_of, (a, b) in zip(x_strips, halves):
        if sh.split:
            strips_of.relay()
            for step in strips_of.rest():
                strips_of.arrival(step)
        lax.fori_loop(a, b, forward, 0)
    gg_home[me] = gg_send[0]
    eo_home[me] = eo_send[0]

    def cotangent_left(step, carry):
        to_plane(c_send.at[0], c_recv.at[0], sh.e_c, step).wait_send()
        return carry

    lax.fori_loop(1, E, cotangent_left, 0)
    ei_send = c_send

    def lanes(c):
        return pl.ds(c * CW, CW)

    for c in range(NC):

        def backward(step, carry):
            if c == 0:
                hid[step] = (nt(delta[step], down[...]) * slope[step]).astype(BF16)
            ei_send[step, :, lanes(c)] = nt(hid[step], up[lanes(c), :]).astype(BF16)

            @pl.when(step > 0)
            def _():
                back_to(
                    ei_send.at[step, :, lanes(c)], ei_home.at[me, :, lanes(c)], sh.e_ei + c, step
                ).start()

            return carry

        lax.fori_loop(0, E, backward, 0)
    ei_home[me] = ei_send[0]

    strip = 128
    F = up.shape[1]
    acc = m.acc

    def flat(ref, first, size):
        return ref[:, :, pl.ds(pl.multiple_of(first, 128), size)].reshape(E * CP, size)

    def strip_copy(i, out, slot):
        return pltpu.make_async_copy(
            acc.at[slot], out.at[pl.ds(pl.multiple_of(i * strip, strip), strip)], local_sem.at[slot]
        )

    def strips(out, lhs, rhs, count, slot):
        def one(i, carry):
            at = slot + lax.rem(i, 2)

            @pl.when(i >= 2)
            def _():
                strip_copy(i - 2, out, at).wait()

            acc[at] = tn(flat(lhs, i * strip, strip), flat(rhs, 0, rhs.shape[2])).astype(BF16)
            strip_copy(i, out, at).start()
            return carry

        lax.fori_loop(0, count, one, 0)

    strips(outputs.up_out, x_recv, hid, D // strip, 0)
    strips(outputs.down_out, act, delta, F // strip, 2)

    for step in range(1, E):
        to_plane(gg_send.at[0], gg_home.at[plane(step)], sh.e_gg, step).wait_recv()

    def pick_dots(e, totals):
        s0, s1 = spread(e)
        column = as_column(gg_home[e][0:1])
        return (
            totals[0] + jnp.sum(jnp.where(s0, column, 0.0), axis=0, keepdims=True),
            totals[1] + jnp.sum(jnp.where(s1, column, 0.0), axis=0, keepdims=True),
        )

    nothing = jnp.zeros((1, RP), F32)
    dots0, dots1 = lax.fori_loop(0, E, pick_dots, (nothing, nothing))
    gz_send, gz_recv = m.gz_send, m.gz_recv
    gz_send[...] = jnp.zeros((8, RP), F32)
    gz_send[0:1] = dots0
    gz_send[1:2] = dots1
    for step in range(1, Z):
        to_depth(gz_send, gz_recv.at[mz], sh.z_gz, step).start()
    mix_part, in_part = m.mix_part, m.in_part
    mix = Scatter(sh.z_mix, mix_part, m.mix_recv, m.mix_pass)
    for step in range(1, E):
        to_plane(eo_send.at[0], eo_home.at[plane(step)], sh.e_eo, step).wait_recv()
    mix_part[...] = nn(place[...], eo_home[...].reshape(E * CP, D)).astype(BF16)
    mix.start()
    mix.relay()
    gate_grad = gz_send[...]
    for step in range(1, Z):
        to_depth(gz_send, gz_recv.at[below(step)], sh.z_gz, step).wait_recv()
        gate_grad = gate_grad + gz_recv[below(step)]
    both = gates[0] * gate_grad[0:1] + gates[1] * gate_grad[1:2]
    logit_grad = sum(hot[k] * (gates[k] * (gate_grad[k : k + 1] - both)) for k in range(2))
    parts = in_three(logit_grad)
    router_grad = sum(nn(p, second_low[...]) for p in parts)
    rterm = m.rterm
    rterm[...] = sum(tn(p, router_t[...]) for p in parts)

    ins = scatters(sh.z_in, in_part, m.in_recv, m.in_pass)
    bo_all, pg_all = m.bo_all, m.pg_all
    bo_gather = windows(sh.z_bo, bo_all)
    for c in range(NC):
        for step in range(1, E):
            to_plane(
                ei_send.at[0, :, lanes(c)], ei_home.at[plane(step), :, lanes(c)], sh.e_ei + c, step
            ).wait_recv()
        home = ei_home[:, :, lanes(c)].reshape(E * CP, CW)
        in_part[c] = nn(place[...], home).astype(BF16)
        ins[c].start()
        if c == 0:
            mixture = mix.total()
            at = lax.broadcasted_iota(jnp.int32, (W, 1), 0) + mz * S
            bo_all[mz] = jnp.where(at < live_rows, resid[window] + mixture, 0.0).astype(BF16)
        ins[c].relay()

    cot = og[window].astype(F32)
    normal, spread_scale = normalize(resid[window])
    second_grad = jnp.concatenate([part.total() for part in ins], axis=1) + rterm[window]
    resid_grad = cot + norm_back(normal, spread_scale, second_grad * g2)
    resid_win = m.resid_win
    resid_win[...] = resid_grad
    attended_grad = jnp.where(own, resid_grad, 0.0).astype(BF16)
    mg_send, mg_recv = m.mg_send, m.mg_recv

    def to_heads(step, sent, received):
        yield to_depth(mg_send.at[sent, tail], mg_recv.at[received, tail], sh.z_mg, step), mz >= 0
        first = to_depth(
            mg_send.at[sent, head], mg_recv.at[received, head], sh.z_mg, step, z_extra
        )
        yield first, received == 0

    def each(found, act):
        for copy, condition in found:

            @pl.when(condition)
            def _():
                act(copy)

    for step in order:
        mg_send[above(step)] = nt(attended_grad, wfull[above(step)]).astype(BF16)
        each(to_heads(step, above(step), mz), lambda c: c.start())
    mg_recv[mz] = nt(attended_grad, wfull[mz]).astype(BF16)
    normal, _ = normalize(resid[...])
    share = jnp.concatenate([in_part[c].astype(F32) for c in range(NC)], axis=1)
    share = share + jnp.where(mz == 0, rterm[...], 0.0)
    m.sp_send[...] = jnp.zeros((sh.small, D), F32)
    m.sp_send[0:E] = jnp.where(mz == 0, router_grad, 0.0)
    m.sp_send[E : E + 1] = jnp.sum(share * normal, axis=0, keepdims=True)
    m.sp_send[E + 1 : E + 2] = jnp.sum(share, axis=0, keepdims=True)

    bo_gather.start()

    B, BP = sh.share, sh.share_rows
    qg = ChipSum(sh.s_qg, m.qg_send, m.qg_pair, m.qg_recv)
    wg = ChipSum(sh.s_og, m.wg_send, m.wg_pair, m.wg_recv)
    lower = mz < Z // 2
    at_rows = pl.ds(pl.multiple_of(lax.rem(mz, Z // 2) * S, TILE), W)
    mixed_win = jnp.concatenate(
        [
            jnp.where(
                lower, mixed_all[p, at_rows][:, 0:L], mixed_all[p, at_rows][:, L : 2 * L]
            )
            for p in range(Z)
        ],
        axis=1,
    )
    wout_grad = tn(attended_grad, mixed_win)
    for e in range(E):
        m.wg_send[e % 2, e // 2, 0:B] = wout_grad[e * B : (e + 1) * B].astype(BF16)
    wg.start()
    for step in order:
        each(to_heads(step, 0, below(step)), lambda c: c.wait_recv())
    wg.cross()
    mixed_grad = m.mixed_grad
    put_together(mg_recv, mixed_grad)

    grads = [[], [], []]
    for h in range(sh.heads):
        mg = mixed_grad[:, h * HEAD_DIM : (h + 1) * HEAD_DIM]
        probs = probs_s[h]
        prob_grad = nt(mg, v_s[h])
        score_grad = (
            probs * (prob_grad - jnp.sum(prob_grad * probs, axis=1, keepdims=True))
        ).astype(BF16)
        grads[0].append((nn(score_grad, k_s[h]) * scale).astype(BF16))
        grads[1].append((tn(score_grad, q_s[h]) * scale).astype(BF16))
        grads[2].append(tn(probs.astype(BF16), mg).astype(BF16))
    projected_grad = jnp.concatenate(grads[0] + grads[1] + grads[2], axis=1)
    mix.finish()
    first_part = mix_part
    first = Scatter(sh.z_first, first_part, m.first_recv, m.first_pass)
    first_part[...] = nn(projected_grad, wqkv[...]).astype(BF16)
    first.start()

    qkv_grad = tn(first_low[...], projected_grad)
    for e in range(E):
        m.qg_send[e % 2, e // 2, 0:B] = qkv_grad[e * B : (e + 1) * B].astype(BF16)
    qg.start()
    normal, _ = normalize(pt[...].astype(F32))
    share = first_part[...].astype(F32)
    m.sp_send[E + 2 : E + 3] = jnp.sum(share * normal, axis=0, keepdims=True)
    m.sp_send[E + 3 : E + 4] = jnp.sum(share, axis=0, keepdims=True)
    smalls = SmallSum(sh.s_sp, m.sp_send, m.sp_pair, m.sp_half, m.sp_recv)
    smalls.start()
    first.relay()
    smalls.cross()

    bo_gather.relay()
    for step in bo_gather.rest():
        bo_gather.arrival(step)
    put_out(bo_all, outputs.block_out, range(Z))

    wz_send, wz_recv = m.wz_send, m.wz_recv
    total_w = wg.total()
    for position in range(Z):
        wz_send[position] = total_w[:, position * L : (position + 1) * L].astype(BF16)
    for step in order:
        to_depth(wz_send.at[above(step)], wz_recv.at[mz], sh.z_wz, step).start()
    zs_send, zs_recv = m.zs_send, m.zs_recv
    near = pl.ds(pl.multiple_of(sh.near(me), 128), sh.near_lanes)
    m.sp_total[...] = smalls.total()
    zs_send[...] = m.sp_total[:, near]
    for step in order:
        to_depth(zs_send, zs_recv.at[mz], sh.z_zs, step).start()

    normal, spread_scale = normalize(pt[window].astype(F32))
    first_grad = first.total()
    patch_grad = resid_win[...] + norm_back(normal, spread_scale, first_grad * g1)
    pg_all[mz] = patch_grad.astype(BF16)
    pg_gather = windows(sh.z_pg, pg_all)
    pg_gather.start()
    qg.cross()
    pg_gather.relay()
    total = qg.total()
    qkv_sum, wout_sum, small_sum = m.qkv_sum, m.wout_sum, m.small_sum
    for part in range(3):
        qkv_sum[part] = total[0:B, part * L : (part + 1) * L]
    store(qkv_sum, outputs.qkv_out)
    total_w = wz_send[mz].astype(F32)
    for step in order:
        to_depth(wz_send.at[0], wz_recv.at[below(step)], sh.z_wz, step).wait_recv()
        total_w = total_w + wz_recv[below(step)].astype(F32)
    wout_sum[...] = total_w[0:B]
    store(wout_sum, outputs.wout_out)
    small_sum[...] = zs_send[...]
    for step in order:
        to_depth(zs_send, zs_recv.at[below(step)], sh.z_zs, step).wait_recv()
        small_sum[...] += zs_recv[below(step)]
    store(small_sum, outputs.small_out)

    for step in (0,) + order:
        position = below(step)
        if step and not (relayed and step == 2):
            pg_gather.arrival(step)
        put_out(pg_all, outputs.patches_grad, [position])

    for step in range(1, Z):
        to_other(step).wait_send()

    def left(step, carry):
        to_plane(g_send.at[0], g_recv.at[0], sh.e_g, step).wait_send()
        common_to(0, step).wait_send()
        if sh.split:
            strip_to(0, step).wait_send()
        back_to(gg_send.at[0], gg_home.at[0], sh.e_gg, step).wait_send()
        back_to(eo_send.at[0], eo_home.at[0], sh.e_eo, step).wait_send()
        for c in range(NC):
            back_to(
                ei_send.at[0, :, lanes(c)], ei_home.at[0, :, lanes(c)], sh.e_ei + c, step
            ).wait_send()
        return carry

    lax.fori_loop(1, E, left, 0)
    for sent in ins + [first, qg, wg, smalls]:
        sent.finish()
    if sh.split:
        for strips_of in x_strips:
            strips_of.finish()
    for gather in (weights, mixing, bo_gather, pg_gather):
        gather.finish()
    for step in range(1, Z):
        each(to_heads(step, 0, mz), lambda c: c.wait_send())
        to_depth(wz_send.at[0], wz_recv.at[0], sh.z_wz, step).wait_send()
        to_depth(gz_send, gz_recv.at[0], sh.z_gz, step).wait_send()
        to_depth(zs_send, zs_recv.at[0], sh.z_zs, step).wait_send()
    for last in (2, 1):
        strip_copy(D // strip - last, outputs.up_out, (D // strip - last) % 2).wait()
        strip_copy(F // strip - last, outputs.down_out, 2 + (F // strip - last) % 2).wait()
    for copy, condition in stores:
        if condition is None:
            copy.wait()
        else:

            @pl.when(condition)
            def _():
                copy.wait()


def scratch_of(sh, F, in_count):
    E, Z, RP, R, D, NC = sh.experts, sh.depth, sh.padded, sh.rows, sh.width, sh.chunks
    CP, CL, CW, W = sh.slots, sh.slot_lanes, sh.chunk, sh.window
    B, BP, C = sh.share, sh.share_rows, sh.chips
    L, H = sh.local, sh.heads
    blocks = ((E, CP, D), BF16)
    dots = ((E, 8, CL), F32)
    rows = ((RP, D), BF16)
    part = ((NC, RP, CW), BF16)
    recv = ((NC, Z, W, CW), BF16)
    passing = ((NC, W, CW), BF16)
    every = ((Z, W, D), BF16)
    head = ((H, RP, HEAD_DIM), BF16)
    shapes = dict(
        gain1=((D,), F32),
        bias1=((D,), F32),
        gain2=((D,), F32),
        bias2=((D,), F32),
        router_t=((E, D), BF16),
        ids_row=((2, R), jnp.int32),
        noise_row=((2, R), F32),
        images_live=((1,), jnp.int32),
        patches=((R, D), BF16),
        out_grad=((R, D), BF16),
        up=((D, F), BF16),
        down=((F, D), BF16),
        wqkv=((3 * L, D), BF16),
        wfull=((Z, L, D), BF16),
        pt=rows,
        og=rows,
        first_low=rows,
        q_s=head,
        k_s=head,
        v_s=head,
        probs_s=((H, RP, RP), F32),
        mixed=((RP, L), BF16),
        mixed_all=((Z, sh.half_rows, 2 * L), BF16),
        resid=((RP, D), F32),
        second_low=rows,
        place=((RP, E * CP), BF16),
        x_send=blocks,
        x_recv=blocks,
        c_send=blocks,
        c_recv=blocks,
        g_send=dots,
        g_recv=dots,
        act=((E, CP, F), BF16),
        slope=((E, CP, F), BF16),
        delta=blocks,
        hid=((E, CP, F), BF16),
        eo_send=blocks,
        eo_home=blocks,
        ei_home=blocks,
        gg_send=dots,
        gg_home=dots,
        acc=((4, 128, max(F, D)), BF16),
        mix_part=rows,
        mix_recv=every,
        mix_pass=((W, D), BF16),
        in_part=part,
        in_recv=recv,
        in_pass=passing,
        first_recv=every,
        first_pass=((W, D), BF16),
        rterm=((RP, D), F32),
        resid_win=((W, D), F32),
        bo_all=every,
        pg_all=every,
        mg_send=((Z, W, L), BF16),
        mg_recv=((Z, W, L), BF16),
        mixed_grad=((RP, L), BF16),
        wz_send=((Z, BP, L), BF16),
        wz_recv=((Z, BP, L), BF16),
        gz_send=((8, RP), F32),
        gz_recv=((Z, 8, RP), F32),
        qg_send=((2, C, BP, 3 * L), BF16),
        qg_pair=((C, BP, 3 * L), BF16),
        qg_recv=((C, BP, 3 * L), BF16),
        wg_send=((2, C, BP, Z * L), BF16),
        wg_pair=((C, BP, Z * L), BF16),
        wg_recv=((C, BP, Z * L), BF16),
        sp_send=((sh.small, D), F32),
        sp_pair=((sh.small, D), F32),
        sp_half=((sh.small, D), F32),
        sp_total=((sh.small, D), F32),
        sp_recv=((C, sh.small, D), F32),
        qkv_sum=((3, B, L), F32),
        wout_sum=((B, L), F32),
        zs_send=((sh.small, sh.near_lanes), F32),
        zs_recv=((Z, sh.small, sh.near_lanes), F32),
        small_sum=((sh.small, sh.near_lanes), F32),
    )
    sems = dict(
        local_sem=4,
        in_sem=in_count,
        out_sem=4 * Z + 3,
        e_sem=(sh.e_kinds, 2, E),
        z_sem=(sh.z_kinds, 2, Z),
        z_extra=(sh.z_kinds, 2, Z),
        s_sem=(sh.s_kinds, 2, Z),
        c_sem=(sh.s_kinds, 2, sh.chips),
    )
    scratch = {field: pltpu.VMEM(*shape) for field, shape in shapes.items()}
    for field, shape in sems.items():
        scratch[field] = pltpu.SemaphoreType.DMA(shape if isinstance(shape, tuple) else (shape,))
    return scratch


def outputs_kernel(sh, pieces, *refs):
    given, outs, held, made = refs[:7], refs[7:18], refs[18:25], refs[25:36]
    in_sem, out_sem = refs[36:]
    wout, small = held[5:]
    loads = [
        pltpu.make_async_copy(src, dst, in_sem.at[at])
        for at, (src, dst) in enumerate(zip(given[5:], (wout, small)))
    ]
    steps = []
    for src, through, ready, dst, number in zip(given, held, made, outs, pieces):
        rows = src.shape[0] // number
        for piece in range(number):
            at = pl.ds(piece * rows, rows)
            part = [ref if number == 1 else ref.at[at] for ref in (src, through, ready, dst)]
            load = pltpu.make_async_copy(part[0], part[1], in_sem.at[len(loads) + len(steps)])
            steps.append((load, part))
    for load in loads + [load for load, _ in steps]:
        load.start()
    for load in loads:
        load.wait()
    E, lanes = sh.experts, sh.near_lanes
    me = lax.axis_index("expert")
    begin = me * sh.share - sh.near(me)
    mine = pltpu.roll(small[...], lax.rem(lanes - begin, lanes), 1)[:, 0 : sh.share]
    made[5][...] = wout[...].T
    made[6][...] = mine[0:E]
    for at, gain in enumerate(made[7:]):
        gain[...] = mine[E + at]
    stores = []

    def store(src, dst):
        stores.append(pltpu.make_async_copy(src, dst, out_sem.at[len(stores)]))
        stores[-1].start()

    for src, dst in zip(made[5:], outs[5:]):
        store(src, dst)
    for load, (_, through, ready, dst) in steps:
        load.wait()
        if through.dtype == ready.dtype:
            store(through, dst)
        else:
            ready[...] = through[...].astype(ready.dtype)
            store(ready, dst)
    for copy in stores:
        copy.wait()


def on_device(
    mesh,
    patches,
    first_gain,
    first_bias,
    qkv_weight,
    out_weight,
    second_gain,
    second_bias,
    router_weight,
    up_weight,
    down_weight,
    expert_ids,
    router_noise,
    images_live,
    out_grad,
):
    row_count, model_width = patches.shape
    local_width = out_weight.shape[0]
    sh = Shapes(mesh, row_count, model_width, local_width)
    hidden_width = up_weight.shape[2]
    E, RP, D = sh.experts, sh.padded, sh.width
    anywhere = pl.BlockSpec(memory_space=pl.ANY)
    slots = E * sh.slots
    flops = 2 * (
        6 * slots * D * hidden_width
        + 3 * RP * D * 4 * local_width
        + 4 * slots * RP * D
        + 7 * sh.heads * RP * RP * HEAD_DIM
    )
    inputs = dict(
        gain1=first_gain,
        bias1=first_bias,
        gain2=second_gain,
        bias2=second_bias,
        router_t=router_weight.T,
        ids_row=expert_ids.T,
        noise_row=router_noise.T,
        images_live=images_live,
        wout=out_weight,
        out_grad=out_grad,
        patches=patches,
        wqkv=qkv_weight.transpose(1, 2, 0).reshape(3 * local_width, D),
        up=up_weight[0],
        down=down_weight[0],
    )
    outputs = dict(
        block_out=jax.ShapeDtypeStruct((RP, D), BF16),
        patches_grad=jax.ShapeDtypeStruct((RP, D), BF16),
        qkv_out=jax.ShapeDtypeStruct((3, sh.share, local_width), F32),
        wout_out=jax.ShapeDtypeStruct((sh.share, local_width), F32),
        small_out=jax.ShapeDtypeStruct((sh.small, sh.near_lanes), F32),
        up_out=jax.ShapeDtypeStruct((D, hidden_width), BF16),
        down_out=jax.ShapeDtypeStruct((hidden_width, D), BF16),
    )
    scratch = scratch_of(sh, hidden_width, len(inputs))
    fields = tuple(tuple(group) for group in (inputs, outputs, scratch))
    outs = pl.pallas_call(
        functools.partial(whole_kernel, sh, fields),
        out_shape=tuple(outputs.values()),
        in_specs=[anywhere] * len(inputs),
        out_specs=(anywhere,) * len(outputs),
        scratch_shapes=list(scratch.values()),
        compiler_params=pltpu.CompilerParams(
            collective_id=0, has_side_effects=True, vmem_limit_bytes=62 << 20
        ),
        cost_estimate=pl.CostEstimate(flops=flops, bytes_accessed=16 << 20, transcendentals=0),
        name="block",
    )(*inputs.values())
    block_out, patches_grad, qkv_grad, wout_grad, small, up_grad, down_grad = outs
    pieces = (1, 1, 1, 4, 4)
    wholes = (block_out[:row_count], patches_grad[:row_count], qkv_grad, up_grad, down_grad)
    inputs = wholes + (wout_grad, small)
    kinds = (BF16, F32, F32, F32, F32)
    results = tuple(jax.ShapeDtypeStruct(w.shape, kind) for w, kind in zip(wholes, kinds)) + (
        jax.ShapeDtypeStruct((local_width, sh.share), F32),
        jax.ShapeDtypeStruct((E, sh.share), F32),
    )
    results += (jax.ShapeDtypeStruct((sh.share,), F32),) * 4
    copies = sum(pieces)
    results = pl.pallas_call(
        functools.partial(outputs_kernel, sh, pieces),
        out_shape=results,
        in_specs=[anywhere] * len(inputs),
        out_specs=(anywhere,) * len(results),
        scratch_shapes=[pltpu.VMEM(w.shape, w.dtype) for w in inputs + results]
        + [pltpu.SemaphoreType.DMA((copies + 2,)), pltpu.SemaphoreType.DMA((copies + 6,))],
        compiler_params=pltpu.CompilerParams(vmem_limit_bytes=62 << 20),
        name="outputs",
    )(*inputs)
    block_out, patches_grad, qkv_grad, up_grad, down_grad, wout_grad, router_grad = results[:7]
    gain2_grad, bias2_grad, gain1_grad, bias1_grad = results[7:]
    return (
        block_out,
        patches_grad,
        gain1_grad,
        bias1_grad,
        qkv_grad.transpose(1, 0, 2),
        wout_grad,
        gain2_grad,
        bias2_grad,
        router_grad.T,
        up_grad[None],
        down_grad[None],
    )


def solution(mesh):
    placed = (
        P("expert", None),
        P(),
        P(),
        P(None, None, "tensor"),
        P("tensor", None),
        P(),
        P(),
        P(),
        P("expert", None, "tensor"),
        P("expert", "tensor", None),
        P("expert", None),
        P("expert", None),
        P("expert"),
        P("expert", None),
    )
    return jax.shard_map(
        functools.partial(on_device, mesh),
        mesh=mesh,
        in_specs=placed,
        out_specs=(
            P("expert", None),
            P("expert", None),
            P("expert"),
            P("expert"),
            P("expert", None, "tensor"),
            P("tensor", "expert"),
            P("expert"),
            P("expert"),
            P("expert", None),
            P("expert", None, "tensor"),
            P("expert", "tensor", None),
        ),
        check_vma=False,
    )
```

time: 158 us -> 154 us (0.975); the launches traced: 158 us -> 152 us
  Pallas kernels: 157 us -> 150 us
    pallas_call x1, Pallas kernels: 152 us -> 146 us  [on_device(): pl.pallas_call(functools.partial(whole_kernel, sh, fields), out_shape=tup...]
where the time goes in v3:
time: 154 us; the launch traced here: 152 us
  Pallas kernels  150 us (97%)
    pallas_call x1, Pallas kernels, on_device(): pl.pallas_call(functools.partial(whole_kernel, sh, fields), out_shape=tup...  146 us
    pallas_call x1, Pallas kernels, on_device(): pl.pallas_call(functools.partial(outputs_kernel, sh, pieces), out_shape=r...  4.31 us

profile of v3, /device:TPU:0, one launch (start us, length us, event | category | flops | bytes accessed | tf_op | source)
XLA Modules:
  0.0 151.8 jit_solution(11993515955558975012)
XLA Ops:
  1.3 146.1 %block.1 = (bf16[400,768]{1,0:T(8,128)(2,1)}, bf16[400,768]{1,0:T(8,128)(2,1)}, f32[3,96,192]{2,1,0:T(8,128)}, f32[96,192]{1,0:T(8,128)}, f32[16,256]{1,0:T(8,12...) custom-call(f32[768]{0:T(1024)} %refs_0_.1, f32[768]{0:T(1024)} %refs_1_.1, f32[768]{0:T(1024)} %refs_2_.1, ...), custom_call_target="tpu_custom_call" | custom-call | flops 14051082240 | bytes 16777216 | tf_op jit(solution)/shard_map/block/pallas_call | solution.py:1278
  147.4 4.3 %outputs.1 = (bf16[394,768]{1,0:T(8,128)(2,1)}, f32[394,768]{1,0:T(8,128)}, f32[3,96,192]{2,1,0:T(8,128)}, f32[768,768]{1,0:T(8,128)}, f32[768,768]{1,0:T(8,128)...) custom-call(bf16[394,768]{1,0:T(8,128)(2,1)} %bitcast.14, ...), custom_call_target="tpu_custom_call" | custom-call | tf_op jit(solution)/shard_map/outputs/pallas_call | solution.py:1301

commit v4 on v3

--- a/solution.py
+++ b/solution.py
@@ -81,11 +81,12 @@
             self.e_c,
             self.e_g,
             self.e_x,
+            self.e_xs,
             self.e_gg,
             self.e_eo,
-            self.e_xs,
             self.e_ei,
         ) = range(7)
+        self.e_single = self.e_gg
         self.e_kinds = self.e_ei + self.chunks
         self.chips = self.experts // 2
         self.s_w, self.s_qg, self.s_og, self.s_sp = range(4)
@@ -94,16 +95,18 @@
             self.z_w,
             self.z_m,
             self.z_gz,
+            self.z_wz,
+            self.z_zs,
+            self.z_x,
+            self.z_y,
             self.z_bo,
             self.z_mg,
-            self.z_wz,
             self.z_pg,
-            self.z_zs,
             self.z_mix,
             self.z_first,
-            self.z_x,
-        ) = range(11)
-        self.z_in = self.z_x + 2
+            self.z_in,
+        ) = range(13)
+        self.z_heads = self.z_bo
         self.z_kinds = self.z_in + self.chunks
 
 
@@ -135,11 +138,18 @@
         return lax.rem(mz - step + Z, Z)
 
     def remote(src, dst, sems, kind, sent, received, expert, position):
+        if sems is e_sem:
+            single = sh.e_single
+            place_of = kind * E + received if kind < single else single * E + kind - single
+            send_sem, recv_sem = m.e_out.at[kind], e_sem.at[place_of]
+        else:
+            row = kind - sh.z_heads if sems is z_extra else kind
+            send_sem, recv_sem = sems.at[row, 0, sent], sems.at[row, 1, received]
         return pltpu.make_async_remote_copy(
             src_ref=src,
             dst_ref=dst,
-            send_sem=sems.at[kind, 0, sent],
-            recv_sem=sems.at[kind, 1, received],
+            send_sem=send_sem,
+            recv_sem=recv_sem,
             device_id=(expert, position),
             device_id_type=MESH,
         )
@@ -769,11 +779,8 @@
     gg_home[me] = gg_send[0]
     eo_home[me] = eo_send[0]
 
-    def cotangent_left(step, carry):
-        to_plane(c_send.at[0], c_recv.at[0], sh.e_c, step).wait_send()
-        return carry
-
-    lax.fori_loop(1, E, cotangent_left, 0)
+    others = pl.ds(0, E - 1)
+    to_plane(c_send.at[others], c_recv.at[others], sh.e_c, 1).wait_send()
     ei_send = c_send
 
     def lanes(c):
@@ -826,8 +833,7 @@
     strips(outputs.up_out, x_recv, hid, D // strip, 0)
     strips(outputs.down_out, act, delta, F // strip, 2)
 
-    for step in range(1, E):
-        to_plane(gg_send.at[0], gg_home.at[plane(step)], sh.e_gg, step).wait_recv()
+    to_plane(gg_send.at[others], gg_home.at[others], sh.e_gg, 1).wait_recv()
 
     def pick_dots(e, totals):
         s0, s1 = spread(e)
@@ -847,8 +853,7 @@
         to_depth(gz_send, gz_recv.at[mz], sh.z_gz, step).start()
     mix_part, in_part = m.mix_part, m.in_part
     mix = Scatter(sh.z_mix, mix_part, m.mix_recv, m.mix_pass)
-    for step in range(1, E):
-        to_plane(eo_send.at[0], eo_home.at[plane(step)], sh.e_eo, step).wait_recv()
+    to_plane(eo_send.at[others], eo_home.at[others], sh.e_eo, 1).wait_recv()
     mix_part[...] = nn(place[...], eo_home[...].reshape(E * CP, D)).astype(BF16)
     mix.start()
     mix.relay()
@@ -867,10 +872,9 @@
     bo_all, pg_all = m.bo_all, m.pg_all
     bo_gather = windows(sh.z_bo, bo_all)
     for c in range(NC):
-        for step in range(1, E):
-            to_plane(
-                ei_send.at[0, :, lanes(c)], ei_home.at[plane(step), :, lanes(c)], sh.e_ei + c, step
-            ).wait_recv()
+        to_plane(
+            ei_send.at[others, :, lanes(c)], ei_home.at[others, :, lanes(c)], sh.e_ei + c, 1
+        ).wait_recv()
         home = ei_home[:, :, lanes(c)].reshape(E * CP, CW)
         in_part[c] = nn(place[...], home).astype(BF16)
         ins[c].start()
@@ -914,8 +918,6 @@
     m.sp_send[0:E] = jnp.where(mz == 0, router_grad, 0.0)
     m.sp_send[E : E + 1] = jnp.sum(share * normal, axis=0, keepdims=True)
     m.sp_send[E + 1 : E + 2] = jnp.sum(share, axis=0, keepdims=True)
-
-    bo_gather.start()
 
     B, BP = sh.share, sh.share_rows
     qg = ChipSum(sh.s_qg, m.qg_send, m.qg_pair, m.qg_recv)
@@ -935,6 +937,7 @@
     for e in range(E):
         m.wg_send[e % 2, e // 2, 0:B] = wout_grad[e * B : (e + 1) * B].astype(BF16)
     wg.start()
+    bo_gather.start()
     for step in order:
         each(to_heads(step, 0, below(step)), lambda c: c.wait_recv())
     wg.cross()
@@ -1024,20 +1027,16 @@
     for step in range(1, Z):
         to_other(step).wait_send()
 
-    def left(step, carry):
-        to_plane(g_send.at[0], g_recv.at[0], sh.e_g, step).wait_send()
-        common_to(0, step).wait_send()
-        if sh.split:
-            strip_to(0, step).wait_send()
-        back_to(gg_send.at[0], gg_home.at[0], sh.e_gg, step).wait_send()
-        back_to(eo_send.at[0], eo_home.at[0], sh.e_eo, step).wait_send()
-        for c in range(NC):
-            back_to(
-                ei_send.at[0, :, lanes(c)], ei_home.at[0, :, lanes(c)], sh.e_ei + c, step
-            ).wait_send()
-        return carry
-
-    lax.fori_loop(1, E, left, 0)
+    to_plane(g_send.at[others], g_recv.at[others], sh.e_g, 1).wait_send()
+    to_plane(x_send.at[others, common], x_recv.at[others, common], sh.e_x, 1).wait_send()
+    if sh.split:
+        rows = split_rows(mz)
+        to_plane(x_send.at[others, rows], x_recv.at[others, rows], sh.e_xs, 1).wait_send()
+    to_plane(gg_send.at[others], gg_home.at[others], sh.e_gg, 1).wait_send()
+    to_plane(eo_send.at[others], eo_home.at[others], sh.e_eo, 1).wait_send()
+    for c in range(NC):
+        part = (others, slice(None), lanes(c))
+        to_plane(ei_send.at[part], ei_home.at[part], sh.e_ei + c, 1).wait_send()
     for sent in ins + [first, qg, wg, smalls]:
         sent.finish()
     if sh.split:
@@ -1159,9 +1158,10 @@
         local_sem=4,
         in_sem=in_count,
         out_sem=4 * Z + 3,
-        e_sem=(sh.e_kinds, 2, E),
+        e_sem=sh.e_single * E + sh.e_kinds - sh.e_single,
+        e_out=sh.e_kinds,
         z_sem=(sh.z_kinds, 2, Z),
-        z_extra=(sh.z_kinds, 2, Z),
+        z_extra=(sh.z_kinds - sh.z_heads, 2, Z),
         s_sem=(sh.s_kinds, 2, Z),
         c_sem=(sh.s_kinds, 2, sh.chips),
     )

time: 154 us -> 151 us (0.981); the launches traced: 152 us -> 151 us
  no operation moved by 1% of the time
where the time goes in v4:
time: 151 us
  Pallas kernels  149 us (99%)
    pallas_call x1, Pallas kernels, on_device(): pl.pallas_call(functools.partial(whole_kernel, sh, fields), out_shape=tup...  145 us
    pallas_call x1, Pallas kernels, on_device(): pl.pallas_call(functools.partial(outputs_kernel, sh, pieces), out_shape=r...  4.31 us

profile of v4, /device:TPU:0, one launch (start us, length us, event | category | flops | bytes accessed | tf_op | source)
XLA Modules:
  0.0 150.9 jit_solution(17583402194051092866)
XLA Ops:
  1.3 145.1 %block.1 = (bf16[400,768]{1,0:T(8,128)(2,1)}, bf16[400,768]{1,0:T(8,128)(2,1)}, f32[3,96,192]{2,1,0:T(8,128)}, f32[96,192]{1,0:T(8,128)}, f32[16,256]{1,0:T(8,12...) custom-call(f32[768]{0:T(1024)} %refs_0_.1, f32[768]{0:T(1024)} %refs_1_.1, f32[768]{0:T(1024)} %refs_2_.1, ...), custom_call_target="tpu_custom_call" | custom-call | flops 14051082240 | bytes 16777216 | tf_op jit(solution)/shard_map/block/pallas_call | solution.py:1278
  146.4 4.3 %outputs.1 = (bf16[394,768]{1,0:T(8,128)(2,1)}, f32[394,768]{1,0:T(8,128)}, f32[3,96,192]{2,1,0:T(8,128)}, f32[768,768]{1,0:T(8,128)}, f32[768,768]{1,0:T(8,128)...) custom-call(bf16[394,768]{1,0:T(8,128)(2,1)} %bitcast.14, ...), custom_call_target="tpu_custom_call" | custom-call | tf_op jit(solution)/shard_map/outputs/pallas_call | solution.py:1301

commit v5 on v4

--- a/solution.py
+++ b/solution.py
@@ -103,11 +103,12 @@
             self.z_mg,
             self.z_pg,
             self.z_mix,
-            self.z_first,
             self.z_in,
-        ) = range(13)
+        ) = range(12)
         self.z_heads = self.z_bo
-        self.z_kinds = self.z_in + self.chunks
+        self.z_first = self.z_in + self.chunks
+        self.z_more = self.z_first + self.chunks
+        self.z_kinds = self.z_more + 1
 
 
     def near(self, expert):
@@ -997,10 +998,15 @@
     first_grad = first.total()
     patch_grad = resid_win[...] + norm_back(normal, spread_scale, first_grad * g1)
     pg_all[mz] = patch_grad.astype(BF16)
-    pg_gather = windows(sh.z_pg, pg_all)
-    pg_gather.start()
+    pg_gathers = []
+    for kind, first_lane in ((sh.z_pg, 0), (sh.z_more, half)):
+        cols = pl.ds(first_lane, half)
+        pg_gathers.append(Gather(kind, pg_all, (tail, cols), (head, cols)))
+    for pg_gather in pg_gathers:
+        pg_gather.start()
     qg.cross()
-    pg_gather.relay()
+    for pg_gather in pg_gathers:
+        pg_gather.relay()
     total = qg.total()
     qkv_sum, wout_sum, small_sum = m.qkv_sum, m.wout_sum, m.small_sum
     for part in range(3):
@@ -1021,7 +1027,8 @@
     for step in (0,) + order:
         position = below(step)
         if step and not (relayed and step == 2):
-            pg_gather.arrival(step)
+            for pg_gather in pg_gathers:
+                pg_gather.arrival(step)
         put_out(pg_all, outputs.patches_grad, [position])
 
     for step in range(1, Z):
@@ -1042,7 +1049,7 @@
     if sh.split:
         for strips_of in x_strips:
             strips_of.finish()
-    for gather in (weights, mixing, bo_gather, pg_gather):
+    for gather in [weights, mixing, bo_gather] + pg_gathers:
         gather.finish()
     for step in range(1, Z):
         each(to_heads(step, 0, mz), lambda c: c.wait_send())

time: 151 us -> 151 us (level)
  no operation moved by 1% of the time
where the time goes in v5:
time: 151 us
  Pallas kernels  149 us (99%)
    pallas_call x1, Pallas kernels, on_device(): pl.pallas_call(functools.partial(whole_kernel, sh, fields), out_shape=tup...  145 us
    pallas_call x1, Pallas kernels, on_device(): pl.pallas_call(functools.partial(outputs_kernel, sh, pieces), out_shape=r...  4.31 us

profile of v5, /device:TPU:0, one launch (start us, length us, event | category | flops | bytes accessed | tf_op | source)
XLA Modules:
  0.0 150.8 jit_solution(13063439894742597871)
XLA Ops:
  1.3 145.0 %block.1 = (bf16[400,768]{1,0:T(8,128)(2,1)}, bf16[400,768]{1,0:T(8,128)(2,1)}, f32[3,96,192]{2,1,0:T(8,128)}, f32[96,192]{1,0:T(8,128)}, f32[16,256]{1,0:T(8,12...) custom-call(f32[768]{0:T(1024)} %refs_0_.1, f32[768]{0:T(1024)} %refs_1_.1, f32[768]{0:T(1024)} %refs_2_.1, ...), custom_call_target="tpu_custom_call" | custom-call | flops 14051082240 | bytes 16777216 | tf_op jit(solution)/shard_map/block/pallas_call | solution.py:1285
  146.3 4.3 %outputs.1 = (bf16[394,768]{1,0:T(8,128)(2,1)}, f32[394,768]{1,0:T(8,128)}, f32[3,96,192]{2,1,0:T(8,128)}, f32[768,768]{1,0:T(8,128)}, f32[768,768]{1,0:T(8,128)...) custom-call(bf16[394,768]{1,0:T(8,128)(2,1)} %bitcast.14, ...), custom_call_target="tpu_custom_call" | custom-call | tf_op jit(solution)/shard_map/outputs/pallas_call | solution.py:1308
